TPU v7x, 32 devices: a whole 2x2x4 slice. The times are simulated.
32 devices in a mesh: blk: 16 (over z, y, x), rep: 2 (over core).
Axes of the slice: x: 2, y: 2, z: 4, core: 2. Of those that a mesh axis runs over, the one named last changes fastest.
Arguments:
- sky_map: float32 [512, 32768], P('blk', 'rep'), may hold values from -6 to 6
- noise_weight: float32 [512, 32768], P('blk', 'rep'), may hold values from 0.25 to 4
- prior_weight: float32 [128, 4, 2, 128], P('blk', 'rep'), may hold values from 0.5 to 4
- seeds: float32 [128, 4, 2, 512], P('blk', 'rep'), may hold values from -5 to 5
- loop_cos: float32 [512], replicated, may hold values from -0.3 to 0.3
- pair_m: int32 [128, 2], replicated, may hold values from 1 to 14939
- block_count: int32 [128], P('blk'), may hold values from 1 to 3, as said below
Outputs:
- solution: float32 [128, 4, 2, 128], P('blk', 'rep')
- residual: float32 [128, 4, 2, 128], P('blk', 'rep')
Inputs may be any that keep to these rules, and one draw needn't show every extreme that they name: `pair_m`: each pair holds two m-columns; values may repeat between pairs. Pair p's first block_count[p] l-blocks belong to its first column, the other 4 - block_count[p] to its second.
All inputs are finite; a program needn't handle non-finite values.
Results may differ from a plain program's by a relative error of at most 0.00045.
Values sent between devices are 32-bit elements; how exact they have to be, the bound alone decides.
A program may use at most 128 MiB of HBM per device.

v0:
```python
import math

import jax
import jax.numpy as jnp
from jax import lax
from jax.sharding import PartitionSpec as P

ITERS = 2


EXACT = lax.Precision.HIGHEST


def block_layout(pair_m, block_count, block_ids):
    block_side = (block_ids[None, :] >= block_count[:, None]).astype(jnp.int32)
    offset = jnp.where(
        block_side == 0, block_ids[None, :], block_ids[None, :] - block_count[:, None]
    )
    column_m = jnp.where(block_side == 0, pair_m[:, 0:1], pair_m[:, 1:2])
    block_start = 128 * (17 * column_m // 2048 + 1) + 128 * offset
    return (block_side, column_m, block_start)


def ladder(degree, column_m):
    degree_f = degree.astype(jnp.float32)
    m_over_l = column_m.astype(jnp.float32) / degree_f
    return jnp.sqrt((4.0 - 1.0 / (degree_f * degree_f)) / ((1.0 - m_over_l) * (1.0 + m_over_l)))


def legendre_rows(column_m, block_start, seeds, loop_cos, visit, initial):
    carried, first_out = visit(initial, seeds[:, 0], 0)
    carried, second_out = visit(carried, seeds[:, 1], 1)

    def advance(packed, step_id):
        earlier, latest, totals = packed
        degree = block_start + step_id
        coef_now = ladder(degree, column_m)[:, None]
        coef_prev = ladder(degree - 1, column_m)[:, None]
        current = coef_now * (loop_cos[None, :] * latest - earlier / coef_prev)
        totals, emitted = visit(totals, current, step_id)
        return ((latest, current, totals), emitted)

    (_, _, carried), others = lax.scan(
        advance, (seeds[:, 0], seeds[:, 1], carried), jnp.arange(2, 128, dtype=jnp.int32), unroll=8
    )
    return (carried, first_out, second_out, others)


def sum_columns(coef, block_side, column_m, block_start, seeds, loop_cos):
    pair_total, block_total = block_side.shape
    count_all = pair_total * block_total
    loop_total = loop_cos.shape[0]
    flat_coef = coef.reshape(count_all, 2, 128)

    def visit(totals, current, step_id):
        weight = lax.dynamic_index_in_dim(flat_coef, step_id, 2, keepdims=False)
        return (totals + weight[:, :, None] * current[:, None, :], None)

    totals, _, _, _ = legendre_rows(
        column_m.reshape(count_all),
        block_start.reshape(count_all),
        seeds.reshape(count_all, 2, loop_total),
        loop_cos,
        visit,
        jnp.zeros((count_all, 2, loop_total), jnp.float32),
    )
    member = (block_side[:, :, None] == jnp.arange(2, dtype=jnp.int32)[None, None, :]).astype(
        jnp.float32
    )
    summed = jnp.einsum(
        "pbs,pbtr->tpsr",
        member,
        totals.reshape(pair_total, block_total, 2, loop_total),
        precision=EXACT,
    )
    return summed.reshape(2, 2 * pair_total, loop_total)


def spread_columns(spectra, block_side, column_m, block_start, seeds, loop_cos):
    pair_total, block_total = block_side.shape
    count_all = pair_total * block_total
    loop_total = loop_cos.shape[0]
    by_side = spectra.reshape(2, pair_total, 2, loop_total)
    side_zero = jnp.transpose(by_side[:, :, 0], (1, 0, 2))[:, None]
    side_one = jnp.transpose(by_side[:, :, 1], (1, 0, 2))[:, None]
    chosen = jnp.where(block_side[:, :, None, None] == 0, side_zero, side_one)
    flat_spec = chosen.reshape(count_all, 2, loop_total)

    def visit(carried, current, step_id):
        return (carried, jnp.sum(current[:, None, :] * flat_spec, axis=2))

    _, first_out, second_out, others = legendre_rows(
        column_m.reshape(count_all),
        block_start.reshape(count_all),
        seeds.reshape(count_all, 2, loop_total),
        loop_cos,
        visit,
        jnp.zeros((), jnp.float32),
    )
    stacked = jnp.concatenate([first_out[None], second_out[None], others], axis=0)
    return jnp.transpose(stacked, (1, 2, 0)).reshape(pair_total, block_total, 2, 128)


def phase_table(every_m, positions, period):
    cycles = positions[:, None] * every_m[None, :] % period
    angles = cycles.astype(jnp.float32) * (2.0 * math.pi / period)
    return (jnp.cos(angles), jnp.sin(angles))


def shards(sky_map, noise_weight, prior_weight, seeds, loop_cos, pair_m, block_count):
    pairs_dev = block_count.shape[0]
    half_blocks = seeds.shape[1]
    loop_total = loop_cos.shape[0]
    columns = 2 * pair_m.shape[0]
    period = sky_map.shape[1] * lax.axis_size("rep")
    map_scale = 1.0 / math.sqrt(loop_total * period)
    rep_index = lax.axis_index("rep")
    local_m = lax.dynamic_slice_in_dim(pair_m, lax.axis_index("blk") * pairs_dev, pairs_dev, 0)
    block_ids = rep_index * half_blocks + jnp.arange(half_blocks, dtype=jnp.int32)
    block_side, column_m, block_start = block_layout(local_m, block_count, block_ids)
    every_m = pair_m.reshape(columns)
    sky_here, noise_here = (sky_map, noise_weight)
    phase_base = rep_index * sky_map.shape[1]
    loop_here, pixel_width = sky_here.shape
    inner_len = min(1024, pixel_width)
    outer_len = pixel_width // inner_len
    cos_inner, sin_inner = phase_table(every_m, jnp.arange(inner_len, dtype=jnp.int32), period)
    basis = jnp.concatenate([cos_inner, sin_inner], axis=1)
    cos_outer, sin_outer = phase_table(
        every_m, phase_base + inner_len * jnp.arange(outer_len, dtype=jnp.int32), period
    )

    def forward(pixels):
        sectioned = jnp.dot(
            pixels.reshape(loop_here * outer_len, inner_len), basis, precision=EXACT
        )
        sectioned = sectioned.reshape(loop_here, outer_len, 2, columns)
        cos_sums, sin_sums = (sectioned[:, :, 0], sectioned[:, :, 1])
        real_part = jnp.einsum("rjm,jm->mr", cos_sums, cos_outer, precision=EXACT) - jnp.einsum(
            "rjm,jm->mr", sin_sums, sin_outer, precision=EXACT
        )
        imag_part = -(
            jnp.einsum("rjm,jm->mr", sin_sums, cos_outer, precision=EXACT)
            + jnp.einsum("rjm,jm->mr", cos_sums, sin_outer, precision=EXACT)
        )
        return map_scale * jnp.stack([real_part, imag_part])

    def analyze(pixels):
        partial_spec = forward(pixels)
        ready = lax.psum(partial_spec, "rep")
        by_column = lax.all_to_all(ready, "blk", split_axis=1, concat_axis=2, tiled=True)
        return spread_columns(by_column, block_side, column_m, block_start, seeds, loop_cos)

    def squares(vector):
        return lax.psum(jnp.sum(vector * vector), ("blk", "rep"))

    rhs_coef = analyze(noise_here * sky_here)
    solution = jnp.zeros_like(rhs_coef)
    residual = rhs_coef
    direction = rhs_coef
    norm_now = squares(residual)
    for turn_id in range(ITERS):
        column_spec = sum_columns(direction, block_side, column_m, block_start, seeds, loop_cos)
        column_spec = lax.psum(column_spec, "rep")
        by_loop = lax.all_to_all(column_spec, "blk", split_axis=2, concat_axis=1, tiled=True)
        spec_re = jnp.transpose(by_loop[0])[:, None, :]
        spec_im = jnp.transpose(by_loop[1])[:, None, :]
        mixed_one = spec_re * cos_outer[None] - spec_im * sin_outer[None]
        mixed_two = spec_re * sin_outer[None] + spec_im * cos_outer[None]
        stacked = jnp.concatenate([mixed_one, -mixed_two], axis=2).reshape(
            loop_here * outer_len, 2 * columns
        )
        inverse_pixels = jnp.einsum("km,jm->kj", stacked, basis, precision=EXACT)
        applied = prior_weight * direction + analyze(
            noise_here * (map_scale * inverse_pixels.reshape(loop_here, pixel_width))
        )
        step_len = norm_now / lax.psum(jnp.sum(direction * applied), ("blk", "rep"))
        solution = solution + step_len * direction
        residual = residual - step_len * applied
        norm_next = squares(residual)
        direction = residual + norm_next / norm_now * direction
        norm_now = norm_next
    return (solution, residual)


def solution(mesh):
    placed = (
        P("blk", "rep"),
        P("blk", "rep"),
        P("blk", "rep", None, None),
        P("blk", "rep", None, None),
        P(),
        P(),
        P("blk"),
    )
    return jax.shard_map(
        shards,
        mesh=mesh,
        in_specs=placed,
        out_specs=(P("blk", "rep", None, None), P("blk", "rep", None, None)),
        check_vma=False,
    )
```

profile of v0, /device:TPU:0, one launch (start us, length us, event | category | flops | bytes accessed | tf_op | source)
XLA Modules:
  0.0 2283.0 jit_solution(11309696597319373117)
XLA Ops:
  8.3 5.6 fusion.156
  57.5 8.3 all-to-all-start
  66.1 7.3 all-to-all-done
  80.3 238.1 %while.95 = (s32[]{:T(128)}, f32[16,512]{1,0:T(8,128)S(1)}, f32[16,512]{1,0:T(8,128)S(1)}, f32[15,8,16,2]{2,3,1,0:T(2,128)}, s32[15,8]{0,1:T(8,128)}, /*index=5*...) while((s32[]{:T(128)}, f32[16,512]{1,0:T(8,128)S(1)}, ...), condition=%wide.region_12.13_spmd.clone.clone, body=%wide.region_3.12_spmd.clone.clone.sunk | while | flops 543474 | bytes 1211981 | solution.py:43
  323.9 599.6 %while.96 = (s32[]{:T(128)}, f32[16,512]{1,0:T(8,128)S(1)}, f32[16,512]{1,0:T(8,128)S(1)}, f32[16,2,512]{2,1,0:T(2,128)S(1)}, s32[15,8]{0,1:T(8,128)}, /*index=5...) while((s32[]{:T(128)}, f32[16,512]{1,0:T(8,128)S(1)}, ...), condition=%wide.region_22.23_spmd.clone.clone, body=%wide.region_21.22_spmd.clone.clone.sunk | while | flops 527370 | bytes 732397 | solution.py:43
  330.0 5.1 fusion.261
  370.0 5.1 fusion.261
  410.0 5.1 fusion.261
  449.9 5.1 fusion.261
  489.9 5.1 fusion.261
  529.9 5.1 fusion.261
  569.8 5.1 fusion.261
  609.8 5.1 fusion.261
  649.8 5.1 fusion.261
  689.8 5.1 fusion.261
  729.7 5.1 fusion.261
  769.7 5.1 fusion.261
  809.7 5.1 fusion.261
  849.6 5.1 fusion.261
  889.6 5.1 fusion.261
  927.6 14.6 all-reduce.9.cloned.1.call-done
  945.7 14.4 all_to_all.75
  966.4 6.1 convolution_multiply_fusion.1
  983.7 14.6 all-reduce.11.cloned.1.call-done
  1000.2 6.8 all-to-all-start.2
  1008.2 6.3 all-to-all-done.2
  1021.0 237.8 %while.97 = (s32[]{:T(128)}, f32[16,512]{1,0:T(8,128)S(1)}, f32[16,512]{1,0:T(8,128)S(1)}, f32[15,8,16,2]{2,3,1,0:T(2,128)}, s32[15,8]{0,1:T(8,128)}, /*index=5*...) while((s32[]{:T(128)}, f32[16,512]{1,0:T(8,128)S(1)}, ...), condition=%wide.region_36.37_spmd.clone.clone, body=%wide.region_27.36_spmd.clone.clone.sunk | while | flops 543474 | bytes 1211981 | solution.py:43
  1265.6 38.6 %all-reduce = (f32[]{:T(128)}, f32[]{:T(128)}) all-reduce(f32[]{:T(128)} %multiply_reduce_fusion.39, f32[]{:T(128)} %multiply_reduce_fusion.38), channel_id=1, replica_groups=mesh['blk'=16,'rep'=2] {'blk','rep'}, use_global_device_ids=true, to_apply=%region_20.21 | all-reduce | flops 2 | bytes 16 | tf_op jit(solution)/shard_map/psum | solution.py:155
  1306.2 40.7 %psum.68 = f32[]{:T(128)} all-reduce(f32[]{:T(128)} %multiply_reduce_fusion.37), channel_id=1, replica_groups=mesh['blk'=16,'rep'=2] {'blk','rep'}, use_global_device_ids=true, to_apply=%region_46.47 | all-reduce | flops 1 | bytes 8 | tf_op jit(solution)/shard_map/psum | solution.py:155
  1350.7 591.8 %while.98 = (s32[]{:T(128)}, f32[16,512]{1,0:T(8,128)S(1)}, f32[16,512]{1,0:T(8,128)S(1)}, f32[16,2,512]{2,1,0:T(2,128)S(1)}, s32[15,8]{0,1:T(8,128)}, /*index=5...) while((s32[]{:T(128)}, f32[16,512]{1,0:T(8,128)S(1)}, ...), condition=%wide.region_48.49_spmd.clone.clone, body=%wide.region_47.48_spmd.clone.clone.sunk | while | flops 527370 | bytes 732397 | solution.py:43
  1356.7 5.0 fusion.268
  1396.1 5.0 fusion.268
  1435.6 5.0 fusion.268
  1475.0 5.0 fusion.268
  1514.5 5.0 fusion.268
  1553.9 5.0 fusion.268
  1593.4 5.0 fusion.268
  1632.9 5.0 fusion.268
  1672.3 5.0 fusion.268
  1711.8 5.0 fusion.268
  1751.2 5.0 fusion.268
  1790.7 5.0 fusion.268
  1954.1 17.7 all-reduce.13.cloned.1.call-done
  1975.3 14.3 all_to_all.76
  1995.1 6.1 convolution_multiply_fusion
  2012.3 14.6 all-reduce.15.cloned.1.call-done
  2028.2 14.3 all_to_all.77
  2044.1 187.7 %while.99 = (s32[]{:T(128)}, f32[16,512]{1,0:T(8,128)S(1)}, f32[16,512]{1,0:T(8,128)S(1)}, f32[15,8,16,2]{2,3,1,0:T(2,128)S(1)}, s32[15,8]{0,1:T(8,128)}, /*inde...) while((s32[]{:T(128)}, f32[16,512]{1,0:T(8,128)S(1)}, ...), condition=%wide.region_62.63_spmd.clone.clone, body=%wide.region_53.62_spmd.clone.clone.sunk | while | flops 543474 | bytes 1218641 | solution.py:43
  2050.2 5.2 fusion.272
  2062.7 5.2 fusion.272
  2075.2 5.2 fusion.272
  2087.7 5.2 fusion.272
  2100.2 5.2 fusion.272
  2112.7 5.2 fusion.272
  2125.2 5.2 fusion.272
  2137.7 5.2 fusion.272
  2150.2 5.2 fusion.272
  2162.8 5.2 fusion.272
  2175.3 5.2 fusion.272
  2187.8 5.2 fusion.272
  2200.3 5.2 fusion.272
  2212.8 5.2 fusion.272
  2225.3 5.2 fusion.272
  2235.7 38.6 %psum.71 = f32[]{:T(128)} all-reduce(f32[]{:T(128)} %multiply_reduce_fusion.36), channel_id=1, replica_groups=mesh['blk'=16,'rep'=2] {'blk','rep'}, use_global_device_ids=true, to_apply=%region_70.71 | all-reduce | flops 1 | bytes 8 | tf_op jit(solution)/shard_map/psum | solution.py:177
  (2355 shorter events, 1316.9 us)
Async XLA Ops:
  7.2 6.8 copy-start
  7.2 46.8 %all-reduce.7.cloned.1.call-start = ((), (), s32[]{:S(2)}) async-start(), calls=%async_computation.5 | async-start | bytes 131072 | tf_op jit(solution)/shard_map/psum | solution.py:150
  19.1 5.5 copy-start.4
  19.1 5.5 copy-start.7
  19.1 1.9 copy-start.1
  21.0 4.7 copy-start.39
  21.0 10.3 copy-start.22
  37.8 280.6 %copy-start.23 = (f32[16]{0:T(128)}, f32[16]{0:T(128)S(1)}, u32[]{:S(2)}) copy-start(f32[16]{0:T(128)S(1)} %get-tuple-element.2190) | copy-start | bytes 196
  37.8 280.6 %copy-start.25 = (f32[16]{0:T(128)}, f32[16]{0:T(128)S(1)}, u32[]{:S(2)}) copy-start(f32[16]{0:T(128)S(1)} %get-tuple-element.2191) | copy-start | bytes 196
  37.8 280.6 %copy-start.27 = (f32[16]{0:T(128)}, f32[16]{0:T(128)S(1)}, u32[]{:S(2)}) copy-start(f32[16]{0:T(128)S(1)} %get-tuple-element.2192) | copy-start | bytes 196
  57.5 15.9 all-to-all-start
  65.8 876.3 %all-reduce.9.cloned.1.call-start = ((), (), s32[]{:S(2)}) async-start(), calls=%async_computation.6 | async-start | bytes 131072 | tf_op jit(solution)/shard_map/psum | solution.py:164
  318.4 3.6 copy-start.20
  925.9 40.4 %copy-start.16 = (f32[16,256]{1,0:T(8,128)S(1)}, f32[16,256]{1,0:T(8,128)}, u32[]{:S(2)}) copy-start(f32[16,256]{1,0:T(8,128)} %get-tuple-element.2184) | copy-start | bytes 49156
  925.9 40.4 %copy-start.18 = (f32[16,256]{1,0:T(8,128)S(1)}, f32[16,256]{1,0:T(8,128)}, u32[]{:S(2)}) copy-start(f32[16,256]{1,0:T(8,128)} %get-tuple-element.2187) | copy-start | bytes 49156
  927.5 70.8 %all-reduce.11.cloned.1.call-start = ((), (), s32[]{:S(2)}) async-start(), calls=%async_computation.7 | async-start | bytes 131072 | tf_op jit(solution)/shard_map/psum | solution.py:150
  978.9 3.6 copy-start.5
  978.9 3.6 copy-start.8
  1000.2 14.3 all-to-all-start.2
  1007.0 964.8 %all-reduce.13.cloned.1.call-start = ((), (), s32[]{:S(2)}) async-start(), calls=%async_computation.8 | async-start | bytes 131072 | tf_op jit(solution)/shard_map/psum | solution.py:164
  1258.8 46.7 %copy-start.12 = (f32[8,2,2,128]{3,2,1,0:T(2,128)S(1)}, f32[8,2,2,128]{3,2,1,0:T(2,128)}, u32[]{:S(2)}) copy-start(f32[8,2,2,128]{3,2,1,0:T(2,128)} %param.19) | copy-start | bytes 49156
  1305.5 45.0 %copy-start.14 = (f32[8,2,2,128]{3,2,1,0:T(2,128)}, f32[8,2,2,128]{3,2,1,0:T(2,128)S(1)}, u32[]{:S(2)}) copy-start(f32[8,2,2,128]{3,2,1,0:T(2,128)S(1)} %multiply_subtract_fusion.3) | copy-start | bytes 49156
  1348.4 2.4 copy-start.10
  1954.0 40.9 %copy-start.17 = (f32[16,256]{1,0:T(8,128)S(1)}, f32[16,256]{1,0:T(8,128)}, u32[]{:S(2)}) copy-start(f32[16,256]{1,0:T(8,128)} %get-tuple-element.2184) | copy-start | bytes 49156
  1954.0 40.9 %copy-start.19 = (f32[16,256]{1,0:T(8,128)S(1)}, f32[16,256]{1,0:T(8,128)}, u32[]{:S(2)}) copy-start(f32[16,256]{1,0:T(8,128)} %get-tuple-element.2187) | copy-start | bytes 49156
  1954.0 72.9 %all-reduce.15.cloned.1.call-start = ((), (), s32[]{:S(2)}) async-start(), calls=%async_computation.9 | async-start | bytes 131072 | tf_op jit(solution)/shard_map/psum | solution.py:150
  2007.6 3.6 copy-start.6
  2007.6 3.6 copy-start.9
  2011.2 32.8 %copy-start.21 = (pred[16]{0:T(512)(128)(4,1)S(1)}, pred[16]{0:T(512)(128)(4,1)}, u32[]{:S(2)}) copy-start(pred[16]{0:T(512)(128)(4,1)} %get-tuple-element.3228) | copy-start | bytes 52
  2043.9 187.8 %copy-start.24 = (f32[16]{0:T(128)S(1)}, f32[16]{0:T(128)}, u32[]{:S(2)}) copy-start(f32[16]{0:T(128)} %copy-done.23) | copy-start | bytes 196
  2043.9 187.8 %copy-start.26 = (f32[16]{0:T(128)S(1)}, f32[16]{0:T(128)}, u32[]{:S(2)}) copy-start(f32[16]{0:T(128)} %copy-done.25) | copy-start | bytes 196
  2043.9 187.8 %copy-start.28 = (f32[16]{0:T(128)S(1)}, f32[16]{0:T(128)}, u32[]{:S(2)}) copy-start(f32[16]{0:T(128)} %copy-done.27) | copy-start | bytes 196
  2044.0 187.8 %copy-start.29 = (f32[16]{0:T(128)S(1)}, f32[16]{0:T(128)}, u32[]{:S(2)}) copy-start(f32[16]{0:T(128)} %get-tuple-element.2193) | copy-start | bytes 196
  2044.0 187.8 %copy-start.30 = (f32[16]{0:T(128)S(1)}, f32[16]{0:T(128)}, u32[]{:S(2)}) copy-start(f32[16]{0:T(128)} %get-tuple-element.2194) | copy-start | bytes 196
  2044.0 187.8 %copy-start.31 = (f32[16]{0:T(128)S(1)}, f32[16]{0:T(128)}, u32[]{:S(2)}) copy-start(f32[16]{0:T(128)} %get-tuple-element.2195) | copy-start | bytes 196
  2044.0 187.8 %copy-start.32 = (f32[16]{0:T(128)S(1)}, f32[16]{0:T(128)}, u32[]{:S(2)}) copy-start(f32[16]{0:T(128)} %get-tuple-element.2196) | copy-start | bytes 196
  2044.0 187.8 %copy-start.33 = (f32[16]{0:T(128)S(1)}, f32[16]{0:T(128)}, u32[]{:S(2)}) copy-start(f32[16]{0:T(128)} %get-tuple-element.2197) | copy-start | bytes 196
  2044.0 187.8 %copy-start.34 = (f32[16]{0:T(128)S(1)}, f32[16]{0:T(128)}, u32[]{:S(2)}) copy-start(f32[16]{0:T(128)} %get-tuple-element.2198) | copy-start | bytes 196
  2044.0 187.8 %copy-start.35 = (f32[16]{0:T(128)S(1)}, f32[16]{0:T(128)}, u32[]{:S(2)}) copy-start(f32[16]{0:T(128)} %get-tuple-element.2199) | copy-start | bytes 196
  2044.0 187.8 %copy-start.36 = (f32[16]{0:T(128)S(1)}, f32[16]{0:T(128)}, u32[]{:S(2)}) copy-start(f32[16]{0:T(128)} %get-tuple-element.2200) | copy-start | bytes 196
  2044.0 187.8 %copy-start.37 = (f32[16]{0:T(128)S(1)}, f32[16]{0:T(128)}, u32[]{:S(2)}) copy-start(f32[16]{0:T(128)} %get-tuple-element.2018) | copy-start | bytes 196
  2044.0 188.9 %copy-start.2 = (f32[8,2,512]{2,0,1:T(8,128)S(1)}, f32[8,2,512]{2,0,1:T(8,128)}, u32[]{:S(2)}) copy-start(f32[8,2,512]{2,0,1:T(8,128)} %copy.794) | copy-start | bytes 98308
  2044.1 188.9 %copy-start.3 = (f32[8,2,512]{2,0,1:T(8,128)S(1)}, f32[8,2,512]{2,0,1:T(8,128)}, u32[]{:S(2)}) copy-start(f32[8,2,512]{2,0,1:T(8,128)} %copy.801) | copy-start | bytes 98308
  2044.1 188.9 %copy-start.38 = (pred[8,2]{0,1:T(4,128)(4,1)S(1)}, pred[8,2]{0,1:T(4,128)(4,1)}, u32[]{:S(2)}) copy-start(pred[8,2]{0,1:T(4,128)(4,1)} %copy.795) | copy-start | bytes 52
  2044.1 190.9 %copy-start.11 = (f32[8,2,2,128]{3,2,1,0:T(2,128)S(1)}, f32[8,2,2,128]{3,2,1,0:T(2,128)}, u32[]{:S(2)}) copy-start(f32[8,2,2,128]{3,2,1,0:T(2,128)} %copy-done.10) | copy-start | bytes 49156
  2044.1 190.9 %copy-start.13 = (f32[8,2,2,128]{3,2,1,0:T(2,128)S(1)}, f32[8,2,2,128]{3,2,1,0:T(2,128)}, u32[]{:S(2)}) copy-start(f32[8,2,2,128]{3,2,1,0:T(2,128)} %param.19) | copy-start | bytes 49156
  2044.1 231.5 %copy-start.15 = (f32[8,2,2,128]{3,2,1,0:T(2,128)S(1)}, f32[8,2,2,128]{3,2,1,0:T(2,128)}, u32[]{:S(2)}) copy-start(f32[8,2,2,128]{3,2,1,0:T(2,128)} %copy-done.14) | copy-start | bytes 49156
Sparse Core Ops, SparseCore 0:
  25.8 20.4 all-reduce.6
  927.6 14.4 all-reduce.8
  983.8 14.4 all-reduce.10
  1954.1 17.5 all-reduce.12
  2012.4 14.4 all-reduce.14
where the time goes:
time: 2320 us; the launch traced here: 2280 us
  local copies, waits for them, and re-layouts  853 us (37%)
  other arithmetic  670 us (29%)
  loops' own time  453 us (20%)
  blocking collectives  161 us (7%)
  waiting for transfers between devices  75.2 us (3%)
  between operations  30.9 us (1%)
  matrix products  24.8 us (1%)
    another operation x5, loops' own time, legendre_rows(): lax.scan(advance, (seeds[:, 0], seeds[:, 1], carried), jnp.arange(2, 128,...  453 us
    sqrt x152, other arithmetic, ladder(): jnp.sqrt((4.0 - 1.0 / (degree_f * degree_f)) / ((1.0 - m_over_l) * (1.0 +...  433 us
    mul x287, local copies, waits for them, and re-layouts, visit(): return (totals + weight[:, :, None] * current[:, None, :], None)  367 us
    broadcast_in_dim x305, local copies, waits for them, and re-layouts, block_layout(): column_m = jnp.where(block_side == 0, pair_m[:, 0:1], pair_m[:, 1:2])  122 us
    ge x306, local copies, waits for them, and re-layouts, block_layout(): block_side = (block_ids[None, :] >= block_count[:, None]).astype(jnp.int32)  119 us
    mul x80, other arithmetic, advance(): current = coef_now * (loop_cos[None, :] * latest - earlier / coef_prev)  83.3 us
    psum x2, blocking collectives, squares(): return lax.psum(jnp.sum(vector * vector), ('blk', 'rep'))  79.3 us
    convert_element_type x75, other arithmetic, ladder(): m_over_l = column_m.astype(jnp.float32) / degree_f  56.1 us
  transfers between devices with their start and end apart: 7, of which 6 were waited for; matrix products, arithmetic and copies ran while one was open for 1% of the time, Pallas kernels for 0%

commit v1 on v0

v1 whole, which is shorter than its diff:
```python
import functools
import math

import jax
import jax.numpy as jnp
from jax import lax
from jax.experimental import pallas as pl
from jax.experimental.pallas import tpu as pltpu
from jax.sharding import PartitionSpec as P

DEG = 128
INNER = 1024
FINE = 32
CHUNK = 8
MESH = pl.DeviceIdType.MESH


def split(x):
    hi = x.astype(jnp.bfloat16)
    return hi, (x - hi.astype(jnp.float32)).astype(jnp.bfloat16)


def kernel(
    nb, scale,
    sky, noise, prior, seeds, lcos, coef_a, coef_b, side,
    cos_a, sin_a, cos_b, sin_b, cos_o, sin_o,
    sol, res,
    legendre, basis_hi, basis_lo, pix_hi, pix_lo, st_hi, st_lo, vecs, send, recv, send_sem, recv_sem,
):
    rows, width = sky.shape
    outer = width // INNER
    cols = cos_o.shape[1]
    pairs = cols // 2
    rings = lcos.shape[1]
    groups = rings // 128
    per = 128 // rows
    n = 2 * nb
    k = lax.axis_index("blk")
    c = lax.axis_index("rep")
    me = c * nb + k
    chunk_rows = CHUNK * rows

    def peer_of(d):
        peer = lax.rem(me + d, n)
        return lax.rem(peer, nb), peer // nb

    barrier = pltpu.get_barrier_semaphore()

    def greet(d, _):
        pk, pc = peer_of(d)
        pl.semaphore_signal(barrier, inc=1, device_id=(pk, pc), device_id_type=MESH)
        return 0

    lax.fori_loop(1, n, greet, 0)

    def post(phase, common):
        def one(d, _):
            pk, pc = peer_of(d)
            pltpu.make_async_remote_copy(
                src_ref=send.at[phase, 0 if common else pk],
                dst_ref=recv.at[phase, me],
                send_sem=send_sem.at[phase],
                recv_sem=recv_sem.at[phase],
                device_id=(pk, pc),
                device_id_type=MESH,
            ).start()
            return 0

        lax.fori_loop(1, n, one, 0)
        recv[phase, me] = send[phase, 0 if common else k]

    def drain(phase, sem):
        block = recv.at[phase, pl.ds(0, n - 1)]
        pltpu.make_async_copy(block, block, sem.at[phase]).wait()

    def make_basis(a, _):
        ca, sa = cos_a[pl.ds(a, 1), :], sin_a[pl.ds(a, 1), :]
        cb, sb = cos_b[...], sin_b[...]
        where = pl.ds(pl.multiple_of(a * FINE, FINE), FINE)
        hi, lo = split(ca * cb - sa * sb)
        basis_hi[where, :cols] = hi
        basis_lo[where, :cols] = lo
        hi, lo = split(sa * cb + ca * sb)
        basis_hi[where, cols:] = hi
        basis_lo[where, cols:] = lo
        return 0

    lax.fori_loop(0, INNER // FINE, make_basis, 0)

    def first_pixels(j, _):
        lanes = pl.ds(pl.multiple_of(j * INNER, INNER), INNER)
        hi, lo = split(sky[:, lanes] * noise[:, lanes])
        where = pl.ds(pl.multiple_of(j * rows, rows), rows)
        pix_hi[where, :] = hi
        pix_lo[where, :] = lo
        return 0

    lax.fori_loop(0, outer, first_pixels, 0)
    vecs[0] = jnp.zeros(vecs.shape[1:], jnp.float32)

    def make_legendre():
        x = jnp.broadcast_to(lcos[...][None], (2, 8, rings))
        wide = lambda a: jnp.concatenate([a] * groups, axis=-1)
        p0, p1 = seeds[0], seeds[1]
        legendre[0] = p0
        legendre[1] = p1

        def advance(i, packed):
            earlier, latest = packed
            now = wide(coef_a[i]) * (x * latest - wide(coef_b[i]) * earlier)
            legendre[i] = now
            return latest, now

        lax.fori_loop(2, DEG, advance, (p0, p1))

    def dots(a_hi, a_lo, b_hi, b_lo, dims):
        dot = functools.partial(
            lax.dot_general, dimension_numbers=dims, preferred_element_type=jnp.float32
        )
        return dot(a_hi, b_hi) + (dot(a_hi, b_lo) + dot(a_lo, b_hi))

    def forward(phase):
        def chunk(h, sums):
            re, im = sums
            where = pl.ds(pl.multiple_of(h * chunk_rows, chunk_rows), chunk_rows)
            sect = dots(
                pix_hi[where, :], pix_lo[where, :], basis_hi[...], basis_lo[...],
                (((1,), (0,)), ((), ())),
            )
            for u in range(CHUNK):
                co = cos_o[pl.ds(h * CHUNK + u, 1), :]
                so = sin_o[pl.ds(h * CHUNK + u, 1), :]
                cs = sect[u * rows:(u + 1) * rows, :cols]
                ss = sect[u * rows:(u + 1) * rows, cols:]
                re = re + (cs * co - ss * so)
                im = im - (ss * co + cs * so)
            return re, im

        zero = jnp.zeros((rows, cols), jnp.float32)
        re, im = lax.fori_loop(0, outer // CHUNK, chunk, (zero, zero))
        stacked = scale * jnp.concatenate(
            [re[:, :pairs], im[:, :pairs], re[:, pairs:], im[:, pairs:]], axis=0
        )
        send[phase] = jnp.transpose(stacked).reshape(nb, 8, 128)

    lane = lax.broadcasted_iota(jnp.int32, (8, 128), 1)

    def spread(phase):
        got = [recv[phase, q] + recv[phase, nb + q] for q in range(nb)]
        gathered = []
        for part in range(4):
            at = part * rows
            gathered.append(
                jnp.concatenate([g[:, at:at + rows] for g in got], axis=1)
            )
        spec = {}
        for b in range(2):
            mask = jnp.concatenate([side[b]] * groups, axis=-1) > 0.5
            for t in range(2):
                spec[t, b] = jnp.where(mask, gathered[2 + t], gathered[t])

        def step(g, acc):
            acc = list(acc)
            for u in range(8):
                i = g * 8 + u
                for b in range(2):
                    leg = legendre[i, b]
                    for t in range(2):
                        prod = leg * spec[t, b]
                        tot = prod[:, :128]
                        for q in range(1, groups):
                            tot = tot + prod[:, q * 128:(q + 1) * 128]
                        val = jnp.sum(tot, axis=1, keepdims=True)
                        acc[2 * t + b] = jnp.where(lane == i, val, acc[2 * t + b])
            return tuple(acc)

        zero = jnp.zeros((8, 128), jnp.float32)
        return lax.fori_loop(0, DEG // 8, step, (zero,) * 4)

    def gather_columns(vec, phase):
        def step(g, packed):
            coef, acc = packed
            acc = list(acc)
            for u in range(8):
                for b in range(2):
                    leg = legendre[g * 8 + u, b]
                    for t in range(2):
                        acc[2 * t + b] = acc[2 * t + b] + leg * coef[2 * t + b][:, u:u + 1]
            coef = tuple(pltpu.roll(x, 120, 1) for x in coef)
            return coef, tuple(acc)

        zero = jnp.zeros((8, rings), jnp.float32)
        _, acc = lax.fori_loop(0, DEG // 8, step, (tuple(vec), (zero,) * 4))
        parts = []
        for s in range(2):
            for t in range(2):
                tot = None
                for b in range(2):
                    mask = jnp.concatenate([side[b]] * groups, axis=-1) > 0.5
                    f = acc[2 * t + b]
                    f = jnp.where(mask, f, 0.0) if s else jnp.where(mask, 0.0, f)
                    tot = f if tot is None else tot + f
                parts.append(tot)
        for q in range(nb):
            send[phase, q] = jnp.concatenate(
                [x[:, q * rows:(q + 1) * rows] for x in parts], axis=1
            )

    def inverse(phase):
        table = (recv[phase, pl.ds(0, nb)] + recv[phase, pl.ds(nb, nb)]).reshape(pairs, 128)
        table = scale * jnp.transpose(table)
        re = jnp.concatenate([table[:rows], table[2 * rows:3 * rows]], axis=1)
        im = jnp.concatenate([table[rows:2 * rows], table[3 * rows:]], axis=1)

        def mix(j, _):
            co, so = cos_o[pl.ds(j, 1), :], sin_o[pl.ds(j, 1), :]
            where = pl.ds(pl.multiple_of(j * rows, rows), rows)
            hi, lo = split(re * co - im * so)
            st_hi[where, :cols] = hi
            st_lo[where, :cols] = lo
            hi, lo = split(-(re * so + im * co))
            st_hi[where, cols:] = hi
            st_lo[where, cols:] = lo
            return 0

        lax.fori_loop(0, outer, mix, 0)

        def chunk(h, _):
            where = pl.ds(pl.multiple_of(h * chunk_rows, chunk_rows), chunk_rows)
            pix = dots(
                st_hi[where, :], st_lo[where, :], basis_hi[...], basis_lo[...],
                (((1,), (1,)), ((), ())),
            )
            for u in range(CHUNK):
                j = h * CHUNK + u
                weight = noise[:, pl.ds(pl.multiple_of(j * INNER, INNER), INNER)]
                hi, lo = split(weight * pix[u * rows:(u + 1) * rows])
                at = pl.ds(pl.multiple_of(j * rows, rows), rows)
                pix_hi[at, :] = hi
                pix_lo[at, :] = lo
            return 0

        lax.fori_loop(0, outer // CHUNK, chunk, 0)

    pl.semaphore_wait(barrier, n - 1)

    def turn(it, _):
        forward(2 * it)
        post(2 * it, False)

        @pl.when(it == 0)
        def _():
            make_legendre()

        drain(2 * it, recv_sem)
        out = spread(2 * it)
        vec = []
        for t in range(2):
            for b in range(2):
                vec.append(prior[t, b] * vecs[it, t, b] + out[2 * t + b])
                vecs[it + 1, t, b] = vec[-1]

        @pl.when(it < 2)
        def _():
            gather_columns(vec, 2 * it + 1)
            post(2 * it + 1, False)
            drain(2 * it + 1, recv_sem)
            inverse(2 * it + 1)

        return 0

    lax.fori_loop(0, 3, turn, 0)

    v0, v1, v2 = vecs[1], vecs[2], vecs[3]

    def partial(a, b):
        x = (a * b).reshape(4, 8, 128)
        return jnp.sum(x[0] + x[1] + (x[2] + x[3]), axis=0, keepdims=True)

    send[5, 0] = jnp.concatenate(
        [partial(v0, v0), partial(v0, v1), partial(v1, v1), partial(v0, v2), partial(v1, v2),
         jnp.zeros((3, 128), jnp.float32)], axis=0
    )
    post(5, True)
    drain(5, recv_sem)
    gram = jnp.sum(jnp.sum(recv[5], axis=0), axis=1, keepdims=True)
    bb, bv, vv, bw, vw = (gram[q:q + 1] for q in range(5))
    alpha = bb / bv
    norm = bb - 2.0 * alpha * bv + alpha * alpha * vv
    beta = norm / bb
    more = 1.0 + beta
    curve = more * more * bv - more * alpha * (bw + vv) + alpha * alpha * vw
    alpha2 = norm / curve
    for t in range(2):
        for b in range(2):
            b0, b1, b2 = v0[t, b], v1[t, b], v2[t, b]
            r1 = b0 - alpha * b1
            d1 = r1 + beta * b0
            sol[t, b] = alpha * b0 + alpha2 * d1
            res[t, b] = r1 - alpha2 * (more * b1 - alpha * b2)

    def finish(phase, _):
        drain(phase, send_sem)
        return 0

    lax.fori_loop(0, 6, finish, 0)


def ladder(degree, column_m):
    degree_f = degree.astype(jnp.float32)
    m_over_l = column_m.astype(jnp.float32) / degree_f
    return jnp.sqrt((4.0 - 1.0 / (degree_f * degree_f)) / ((1.0 - m_over_l) * (1.0 + m_over_l)))


def phases(every_m, positions, period):
    cycles = positions[:, None] * every_m[None, :]
    if period & (period - 1) == 0:
        cycles = cycles & (period - 1)
    else:
        cycles = cycles % period
    angles = cycles.astype(jnp.float32) * (2.0 * math.pi / period)
    return jnp.cos(angles), jnp.sin(angles)


def shards(sky_map, noise_weight, prior_weight, seeds, loop_cos, pair_m, block_count):
    nb = lax.axis_size("blk")
    pairs_dev = block_count.shape[0]
    half = seeds.shape[1]
    rings = loop_cos.shape[0]
    cols = 2 * pair_m.shape[0]
    rows, width = sky_map.shape
    period = width * lax.axis_size("rep")
    scale = 1.0 / math.sqrt(rings * period)
    rep = lax.axis_index("rep")
    local_m = lax.dynamic_slice_in_dim(pair_m, lax.axis_index("blk") * pairs_dev, pairs_dev, 0)
    ids = rep * half + jnp.arange(half, dtype=jnp.int32)[:, None]
    on_second = ids >= block_count[None, :]
    offset = jnp.where(on_second, ids - block_count[None, :], ids)
    column_m = jnp.where(on_second, local_m[None, :, 1], local_m[None, :, 0])
    start = 128 * (17 * column_m // 2048 + 1) + 128 * offset
    degree = start[None] + jnp.arange(DEG, dtype=jnp.int32)[:, None, None]
    big = (DEG, half, pairs_dev, 128)
    coef_a = jnp.broadcast_to(ladder(degree, column_m[None])[..., None], big)
    coef_b = jnp.broadcast_to((1.0 / ladder(degree - 1, column_m[None]))[..., None], big)
    side = jnp.broadcast_to(on_second.astype(jnp.float32)[..., None], big[1:])
    every_m = jnp.transpose(pair_m).reshape(cols)
    outer = width // INNER
    coarse = INNER // FINE
    fine_at = jnp.arange(FINE, dtype=jnp.int32)
    coarse_at = FINE * jnp.arange(coarse, dtype=jnp.int32)
    outer_at = rep * width + INNER * jnp.arange(outer, dtype=jnp.int32)
    cos_all, sin_all = phases(every_m, jnp.concatenate([coarse_at, fine_at, outer_at]), period)
    cut = lambda a: (a[:coarse], a[coarse:coarse + FINE], a[coarse + FINE:])
    cos_a, cos_b, cos_o = cut(cos_all)
    sin_a, sin_b, sin_o = cut(sin_all)
    vmem = pl.BlockSpec(memory_space=pltpu.VMEM)
    out = jax.ShapeDtypeStruct((2, half, pairs_dev, DEG), jnp.float32)
    sol, res = pl.pallas_call(
        functools.partial(kernel, nb, scale),
        out_shape=(out, out),
        in_specs=[vmem] * 14,
        out_specs=(vmem, vmem),
        scratch_shapes=[
            pltpu.VMEM((DEG, half, pairs_dev, rings), jnp.float32),
            pltpu.VMEM((INNER, 2 * cols), jnp.bfloat16),
            pltpu.VMEM((INNER, 2 * cols), jnp.bfloat16),
            pltpu.VMEM((outer * rows, INNER), jnp.bfloat16),
            pltpu.VMEM((outer * rows, INNER), jnp.bfloat16),
            pltpu.VMEM((outer * rows, 2 * cols), jnp.bfloat16),
            pltpu.VMEM((outer * rows, 2 * cols), jnp.bfloat16),
            pltpu.VMEM((4, 2, half, pairs_dev, DEG), jnp.float32),
            pltpu.VMEM((6, nb, 8, 128), jnp.float32),
            pltpu.VMEM((6, 2 * nb, 8, 128), jnp.float32),
            pltpu.SemaphoreType.DMA((6,)),
            pltpu.SemaphoreType.DMA((6,)),
        ],
        compiler_params=pltpu.CompilerParams(
            collective_id=0, has_side_effects=True, vmem_limit_bytes=58 * 2**20
        ),
        name="wiener",
    )(
        sky_map, noise_weight,
        jnp.transpose(prior_weight, (2, 1, 0, 3)),
        jnp.transpose(seeds, (2, 1, 0, 3)),
        loop_cos[None, :],
        coef_a, coef_b, side, cos_a, sin_a, cos_b, sin_b, cos_o, sin_o,
    )
    back = lambda a: jnp.transpose(a, (2, 1, 0, 3))
    return back(sol), back(res)


def solution(mesh):
    placed = (
        P("blk", "rep"),
        P("blk", "rep"),
        P("blk", "rep", None, None),
        P("blk", "rep", None, None),
        P(),
        P(),
        P("blk"),
    )
    return jax.shard_map(
        shards,
        mesh=mesh,
        in_specs=placed,
        out_specs=(P("blk", "rep", None, None), P("blk", "rep", None, None)),
        check_vma=False,
    )
```

time: 2320 us -> 76 us (0.03); the launches traced: 2280 us -> 75.6 us
  local copies, waits for them, and re-layouts: 853 us -> 10.2 us
  other arithmetic: 670 us -> 1.37 us
  loops' own time: 453 us -> 0 us
  blocking collectives: 161 us -> 0 us
  waiting for transfers between devices: 75.2 us -> 0 us
  Pallas kernels: 0 us -> 63.4 us
  between operations: 30.9 us -> 0.71 us
  matrix products: 24.8 us -> 0 us
    another operation x5 -> x0, loops' own time: 453 us -> none  [legendre_rows(): lax.scan(advance, (seeds[:, 0], seeds[:, 1], carried), jnp.arange(2, 128,...]
    sqrt x152 -> x1, other arithmetic: 433 us -> 0.1 us  [ladder(): jnp.sqrt((4.0 - 1.0 / (degree_f * degree_f)) / ((1.0 - m_over_l) * (1.0 +...]
    mul x330 -> x0, local copies, waits for them, and re-layouts: 375 us -> none  [the longest x287 367 us: visit(): return (totals + weight[:, :, None] * current[:, None, :], None)]
    broadcast_in_dim x525 -> x4, local copies, waits for them, and re-layouts: 178 us -> 3.34 us  [the longest x1 1.36 us: shards(): jnp.broadcast_to((1.0 / ladder(degree - 1, column_m[None]))[..., None], big)]
    ge x306 -> x0, local copies, waits for them, and re-layouts: 119 us -> none  [block_layout(): block_side = (block_ids[None, :] >= block_count[:, None]).astype(jnp.int32)]
    psum x3 -> x0, blocking collectives: 118 us -> none  [the longest x2 79.3 us: squares(): return lax.psum(jnp.sum(vector * vector), ('blk', 'rep'))]
    mul x86 -> x1, other arithmetic: 91.8 us -> 0.01 us  [shards(): coarse_at = FINE * jnp.arange(coarse, dtype=jnp.int32)]
    pallas_call x0 -> x1, Pallas kernels: none -> 63.4 us  [shards(): pl.pallas_call(functools.partial(kernel, nb, scale), out_shape=(out, out)...]
  transfers between devices with their start and end apart: 7 -> 0, of which waited for: 6 -> 0; matrix products, arithmetic and copies ran while one was open for 1% -> 0% of each run, Pallas kernels for 0% -> 0%
where the time goes in v1:
time: 76 us; the launch traced here: 75.6 us
  Pallas kernels  63.4 us (83%)
  local copies, waits for them, and re-layouts  10.2 us (13%)
  other arithmetic  1.37 us (2%)
    pallas_call x1, Pallas kernels, shards(): pl.pallas_call(functools.partial(kernel, nb, scale), out_shape=(out, out)...  63.4 us
    unnamed x12, local copies, waits for them, and re-layouts  3.93 us
    slice x3, local copies, waits for them, and re-layouts, shards(): cut = lambda a: (a[:coarse], a[coarse:coarse + FINE], a[coarse + FINE:])  1.86 us

profile of v1, /device:TPU:0, one launch (start us, length us, event | category | flops | bytes accessed | tf_op | source)
XLA Modules:
  0.0 75.6 jit_solution(14687853336042733109)
XLA Ops:
  0.6 0.0 copy-start.2
  0.6 0.0 copy-start.3
  0.7 0.0 copy-start
  0.7 0.0 copy-start.1
  0.7 0.8 %constant_dynamic-slice_fusion = s32[8,2]{0,1:T(2,128)S(1)} fusion(s32[128,2]{0,1:T(2,128)} %param.12, s32[]{:T(128)S(6)} %select_n.31), kind=kLoop, calls=%fused_computation.25 | loop fusion | bytes 132 | tf_op jit(solution)/shard_map/dynamic_slice | solution.py:335
  1.5 0.7 fusion.5
  2.2 0.1 divide_rsqrt_fusion
  2.3 0.1 copy.15
  2.5 1.3 %broadcast_in_dim.60.coef_a = f32[128,2,8,128]{3,2,1,0:T(8,128)} broadcast(f32[128,2,8]{2,1,0:T(2,128)S(1)} %copy.15), dimensions={0,1,2} | broadcast | bytes 1056768 | tf_op jit(solution)/shard_map/broadcast_in_dim | solution.py:343
  3.8 0.1 copy.16
  3.9 1.4 %broadcast_in_dim.61.coef_b = f32[128,2,8,128]{3,2,1,0:T(8,128)} broadcast(f32[128,2,8]{2,1,0:T(2,128)S(1)} %copy.16), dimensions={0,1,2} | broadcast | bytes 1056768 | tf_op jit(solution)/shard_map/broadcast_in_dim | solution.py:344
  5.3 0.1 pad_add_fusion
  5.4 0.0 copy-done.2
  5.4 0.4 fusion
  5.7 0.7 fusion.6
  6.4 0.6 slice.36.cos_o
  7.0 0.6 slice.37.sin_o
  7.6 0.0 copy-done.3
  7.6 0.1 compare_convert_fusion
  7.7 0.7 broadcast_in_dim.62.side
  8.3 0.0 copy-done
  8.3 0.6 copy.21
  9.0 0.0 copy-done.1
  9.0 0.6 copy.22
  9.6 63.4 %wiener.1 = (f32[2,2,8,128]{3,2,1,0:T(8,128)}, f32[2,2,8,128]{3,2,1,0:T(8,128)}) custom-call(f32[32,16384]{1,0:T(8,128)} %sky.1, f32[32,16384]{1,0:T(8,128)} %noise.1, f32[2,2,8,128]{3,2,1,0:T(8,128)} %bitcast.17, f32[2,2,8,512]{3,2,1,0:T(8,128)} %bitcast.16, f32[1,512]{1,0:T(1,128)} %bitcast.21, f32[128,2,8,128]{3,2,1,0:T(8,128)} %broadcast_in_dim.60.coef_a, ...), custom_call_target="tpu_custom_call" | custom-call | tf_op jit(solution)/shard_map/wiener/pallas_call | solution.py:358
  73.0 1.3 %copy.17 = f32[8,2,2,128]{3,2,1,0:T(2,128)} copy(f32[8,2,2,128]{3,0,1,2:T(8,128)} %bitcast.19) | data formatting | bytes 32768
  74.3 1.3 %copy.18 = f32[8,2,2,128]{3,2,1,0:T(2,128)} copy(f32[8,2,2,128]{3,0,1,2:T(8,128)} %bitcast.18) | data formatting | bytes 32768
  (5 shorter events, 0.0 us)
Async XLA Ops:
  0.6 4.7 %copy-start.2 = (s32[128,2]{0,1:T(2,128)S(1)}, s32[128,2]{0,1:T(2,128)}, u32[]{:S(2)}) copy-start(s32[128,2]{0,1:T(2,128)} %param.12) | copy-start | bytes 3076
  0.6 7.0 %copy-start.3 = (s32[8]{0:T(128)S(1)}, s32[8]{0:T(128)}, u32[]{:S(2)}) copy-start(s32[8]{0:T(128)} %param.13) | copy-start | bytes 100
  0.7 7.7 %copy-start = (f32[8,2,2,512]{3,2,1,0:T(2,128)S(1)}, f32[8,2,2,512]{3,2,1,0:T(2,128)}, u32[]{:S(2)}) copy-start(f32[8,2,2,512]{3,2,1,0:T(2,128)} %param.10) | copy-start | bytes 196612
  0.7 8.3 %copy-start.1 = (f32[8,2,2,128]{3,2,1,0:T(2,128)S(1)}, f32[8,2,2,128]{3,2,1,0:T(2,128)}, u32[]{:S(2)}) copy-start(f32[8,2,2,128]{3,2,1,0:T(2,128)} %param.9) | copy-start | bytes 49156

commit v2 on v1

--- a/solution.py
+++ b/solution.py
@@ -21,16 +21,18 @@
 
 
 def kernel(
-    nb, scale,
-    sky, noise, prior, seeds, lcos, coef_a, coef_b, side,
-    cos_a, sin_a, cos_b, sin_b, cos_o, sin_o,
+    nb, scale, period,
+    sky_in, noise_in, prior_in, seeds, lcos, every_m, counts,
     sol, res,
-    legendre, basis_hi, basis_lo, pix_hi, pix_lo, st_hi, st_lo, vecs, send, recv, send_sem, recv_sem,
+    sky, noise, legendre, basis_hi, basis_lo, pix_hi, pix_lo, st_hi, st_lo,
+    cos_a, sin_a, cos_b, sin_b, cos_o, sin_o, by_pair, side, prior,
+    vecs, send, recv, load_sem, send_sem, recv_sem,
 ):
     rows, width = sky.shape
     outer = width // INNER
     cols = cos_o.shape[1]
     pairs = cols // 2
+    half = side.shape[0]
     rings = lcos.shape[1]
     groups = rings // 128
     per = 128 // rows
@@ -44,6 +46,12 @@
         peer = lax.rem(me + d, n)
         return lax.rem(peer, nb), peer // nb
 
+    loads = [
+        pltpu.make_async_copy(sky_in, sky, load_sem.at[0]),
+        pltpu.make_async_copy(noise_in, noise, load_sem.at[1]),
+    ]
+    for load in loads:
+        load.start()
     barrier = pltpu.get_barrier_semaphore()
 
     def greet(d, _):
@@ -73,6 +81,16 @@
         block = recv.at[phase, pl.ds(0, n - 1)]
         pltpu.make_async_copy(block, block, sem.at[phase]).wait()
 
+    m_row = jnp.concatenate([every_m[0:1, :], every_m[1:2, :]], axis=1)
+
+    def trig(count, base, step, cos_ref, sin_ref):
+        at = base + step * lax.broadcasted_iota(jnp.int32, (count, cols), 0)
+        cos_ref[...], sin_ref[...] = phases(at * m_row, period)
+
+    trig(INNER // FINE, 0, FINE, cos_a, sin_a)
+    trig(FINE, 0, 1, cos_b, sin_b)
+    trig(outer, c * width, INNER, cos_o, sin_o)
+
     def make_basis(a, _):
         ca, sa = cos_a[pl.ds(a, 1), :], sin_a[pl.ds(a, 1), :]
         cb, sb = cos_b[...], sin_b[...]
@@ -87,6 +105,9 @@
 
     lax.fori_loop(0, INNER // FINE, make_basis, 0)
 
+    for load in loads:
+        load.wait()
+
     def first_pixels(j, _):
         lanes = pl.ds(pl.multiple_of(j * INNER, INNER), INNER)
         hi, lo = split(sky[:, lanes] * noise[:, lanes])
@@ -98,20 +119,67 @@
     lax.fori_loop(0, outer, first_pixels, 0)
     vecs[0] = jnp.zeros(vecs.shape[1:], jnp.float32)
 
+    row_id = lax.broadcasted_iota(jnp.int32, (8, 128), 0)
+    lane = lax.broadcasted_iota(jnp.int32, (8, 128), 1)
+
     def make_legendre():
-        x = jnp.broadcast_to(lcos[...][None], (2, 8, rings))
-        wide = lambda a: jnp.concatenate([a] * groups, axis=-1)
-        p0, p1 = seeds[0], seeds[1]
-        legendre[0] = p0
-        legendre[1] = p1
-
-        def advance(i, packed):
-            earlier, latest = packed
-            now = wide(coef_a[i]) * (x * latest - wide(coef_b[i]) * earlier)
-            legendre[i] = now
-            return latest, now
-
-        lax.fori_loop(2, DEG, advance, (p0, p1))
+        m_float = every_m[...].astype(jnp.float32)
+        by_pair[...] = jnp.transpose(
+            jnp.concatenate([m_float, jnp.zeros((126, pairs), jnp.float32)], axis=0)
+        )
+        mine = by_pair[pl.ds(pl.multiple_of(k * 8, 8), 8), :]
+        m_first = jnp.broadcast_to(mine[:, 0:1], (8, 128)).astype(jnp.int32)
+        m_second = jnp.broadcast_to(mine[:, 1:2], (8, 128)).astype(jnp.int32)
+        count = jnp.zeros((8, 128), jnp.int32)
+        for p in range(8):
+            count = jnp.where(row_id == p, counts[p], count)
+        coefs = []
+        for b in range(half):
+            block = c * half + b
+            second = count <= block
+            offset = jnp.where(second, block - count, block)
+            column = jnp.where(second, m_second, m_first)
+            degree = 128 * (lax.shift_right_logical(17 * column, 11) + 1) + 128 * offset + lane
+            coefs.append((ladder(degree, column), 1.0 / ladder(degree - 1, column)))
+            side[b] = jnp.where(second, 1.0, 0.0)
+            for t in range(2):
+                prior[t, b] = jnp.concatenate(
+                    [prior_in[p, b, t:t + 1, :] for p in range(8)], axis=0
+                )
+        x = jnp.broadcast_to(lcos[...], (8, rings))
+        wide = lambda a, u: jnp.concatenate(
+            [jnp.broadcast_to(a[:, u:u + 1], (8, 128))] * groups, axis=-1
+        )
+        state = []
+        for b in range(half):
+            for i in range(2):
+                state.append(
+                    jnp.concatenate([seeds[p, b, i:i + 1, :] for p in range(8)], axis=0)
+                )
+                legendre[i, b] = state[-1]
+
+        def advance(i, u, coefs, state):
+            out = []
+            for b in range(half):
+                earlier, latest = state[2 * b:2 * b + 2]
+                ca, cb = coefs[2 * b:2 * b + 2]
+                now = wide(ca, u) * (x * latest - wide(cb, u) * earlier)
+                legendre[i, b] = now
+                out += [latest, now]
+            return out
+
+        coefs = [v for pair in coefs for v in pair]
+        for i in range(2, 8):
+            state = advance(i, i, coefs, state)
+
+        def step(g, packed):
+            coefs, state = packed
+            coefs = tuple(pltpu.roll(v, 120, 1) for v in coefs)
+            for u in range(8):
+                state = advance(g * 8 + u, u, coefs, state)
+            return coefs, tuple(state)
+
+        lax.fori_loop(1, DEG // 8, step, (tuple(coefs), tuple(state)))
 
     def dots(a_hi, a_lo, b_hi, b_lo, dims):
         dot = functools.partial(
@@ -143,8 +211,6 @@
         )
         send[phase] = jnp.transpose(stacked).reshape(nb, 8, 128)
 
-    lane = lax.broadcasted_iota(jnp.int32, (8, 128), 1)
-
     def spread(phase):
         got = [recv[phase, q] + recv[phase, nb + q] for q in range(nb)]
         gathered = []
@@ -225,7 +291,7 @@
 
         lax.fori_loop(0, outer, mix, 0)
 
-        def chunk(h, _):
+        def chunk(h, energy):
             where = pl.ds(pl.multiple_of(h * chunk_rows, chunk_rows), chunk_rows)
             pix = dots(
                 st_hi[where, :], st_lo[where, :], basis_hi[...], basis_lo[...],
@@ -234,13 +300,22 @@
             for u in range(CHUNK):
                 j = h * CHUNK + u
                 weight = noise[:, pl.ds(pl.multiple_of(j * INNER, INNER), INNER)]
-                hi, lo = split(weight * pix[u * rows:(u + 1) * rows])
+                values = pix[u * rows:(u + 1) * rows]
+                weighted = weight * values
+                power = weighted * values
+                for q in range(INNER // 128):
+                    energy = energy + power[:, q * 128:(q + 1) * 128]
+                hi, lo = split(weighted)
                 at = pl.ds(pl.multiple_of(j * rows, rows), rows)
                 pix_hi[at, :] = hi
                 pix_lo[at, :] = lo
-            return 0
-
-        lax.fori_loop(0, outer // CHUNK, chunk, 0)
+            return energy
+
+        return lax.fori_loop(0, outer // CHUNK, chunk, jnp.zeros((rows, 128), jnp.float32))
+
+    def dot_lanes(a, b):
+        x = (a * b).reshape(4, 8, 128)
+        return jnp.sum(x[0] + x[1] + (x[2] + x[3]), axis=0, keepdims=True)
 
     pl.semaphore_wait(barrier, n - 1)
 
@@ -265,7 +340,17 @@
             gather_columns(vec, 2 * it + 1)
             post(2 * it + 1, False)
             drain(2 * it + 1, recv_sem)
-            inverse(2 * it + 1)
+            energy = inverse(2 * it + 1)
+
+            @pl.when(it == 1)
+            def _():
+                v0, v1 = vecs[1], vecs[2]
+                bent = dot_lanes(v1, prior[...] * v1) + jnp.sum(energy, axis=0, keepdims=True)
+                send[5, 0] = jnp.concatenate(
+                    [dot_lanes(v0, v0), dot_lanes(v0, v1), dot_lanes(v1, v1), bent,
+                     jnp.zeros((4, 128), jnp.float32)], axis=0
+                )
+                post(5, True)
 
         return 0
 
@@ -273,31 +358,25 @@
 
     v0, v1, v2 = vecs[1], vecs[2], vecs[3]
 
-    def partial(a, b):
-        x = (a * b).reshape(4, 8, 128)
-        return jnp.sum(x[0] + x[1] + (x[2] + x[3]), axis=0, keepdims=True)
-
-    send[5, 0] = jnp.concatenate(
-        [partial(v0, v0), partial(v0, v1), partial(v1, v1), partial(v0, v2), partial(v1, v2),
-         jnp.zeros((3, 128), jnp.float32)], axis=0
-    )
-    post(5, True)
     drain(5, recv_sem)
     gram = jnp.sum(jnp.sum(recv[5], axis=0), axis=1, keepdims=True)
-    bb, bv, vv, bw, vw = (gram[q:q + 1] for q in range(5))
+    bb, bv, vv, vw = (gram[q:q + 1] for q in range(4))
     alpha = bb / bv
     norm = bb - 2.0 * alpha * bv + alpha * alpha * vv
     beta = norm / bb
     more = 1.0 + beta
-    curve = more * more * bv - more * alpha * (bw + vv) + alpha * alpha * vw
+    curve = more * more * bv - 2.0 * more * alpha * vv + alpha * alpha * vw
     alpha2 = norm / curve
     for t in range(2):
         for b in range(2):
             b0, b1, b2 = v0[t, b], v1[t, b], v2[t, b]
             r1 = b0 - alpha * b1
             d1 = r1 + beta * b0
-            sol[t, b] = alpha * b0 + alpha2 * d1
-            res[t, b] = r1 - alpha2 * (more * b1 - alpha * b2)
+            found = alpha * b0 + alpha2 * d1
+            left = r1 - alpha2 * (more * b1 - alpha * b2)
+            for p in range(8):
+                sol[p, b, t:t + 1, :] = found[p:p + 1]
+                res[p, b, t:t + 1, :] = left[p:p + 1]
 
     def finish(phase, _):
         drain(phase, send_sem)
@@ -312,14 +391,24 @@
     return jnp.sqrt((4.0 - 1.0 / (degree_f * degree_f)) / ((1.0 - m_over_l) * (1.0 + m_over_l)))
 
 
-def phases(every_m, positions, period):
-    cycles = positions[:, None] * every_m[None, :]
+def phases(cycles, period):
+    quarter = period // 4
     if period & (period - 1) == 0:
         cycles = cycles & (period - 1)
+        turn = lax.shift_right_logical(cycles + quarter // 2, quarter.bit_length() - 1)
     else:
-        cycles = cycles % period
-    angles = cycles.astype(jnp.float32) * (2.0 * math.pi / period)
-    return jnp.cos(angles), jnp.sin(angles)
+        cycles = lax.rem(cycles, period)
+        turn = lax.div(cycles + quarter // 2, quarter)
+    x = (cycles - quarter * turn).astype(jnp.float32) * (2.0 * math.pi / period)
+    y = x * x
+    sin = x * (1 + y * (-1 / 6 + y * (1 / 120 + y * (-1 / 5040 + y * (1 / 362880)))))
+    cos = 1 + y * (-1 / 2 + y * (1 / 24 + y * (-1 / 720 + y * (1 / 40320 - y * (1 / 3628800)))))
+    odd = (turn & 1) == 1
+    cos_abs, sin_abs = jnp.where(odd, sin, cos), jnp.where(odd, cos, sin)
+    return (
+        jnp.where(((turn + 1) & 2) == 2, -cos_abs, cos_abs),
+        jnp.where((turn & 2) == 2, -sin_abs, sin_abs),
+    )
 
 
 def shards(sky_map, noise_weight, prior_weight, seeds, loop_cos, pair_m, block_count):
@@ -327,50 +416,46 @@
     pairs_dev = block_count.shape[0]
     half = seeds.shape[1]
     rings = loop_cos.shape[0]
-    cols = 2 * pair_m.shape[0]
+    pairs = pair_m.shape[0]
+    cols = 2 * pairs
     rows, width = sky_map.shape
     period = width * lax.axis_size("rep")
     scale = 1.0 / math.sqrt(rings * period)
-    rep = lax.axis_index("rep")
-    local_m = lax.dynamic_slice_in_dim(pair_m, lax.axis_index("blk") * pairs_dev, pairs_dev, 0)
-    ids = rep * half + jnp.arange(half, dtype=jnp.int32)[:, None]
-    on_second = ids >= block_count[None, :]
-    offset = jnp.where(on_second, ids - block_count[None, :], ids)
-    column_m = jnp.where(on_second, local_m[None, :, 1], local_m[None, :, 0])
-    start = 128 * (17 * column_m // 2048 + 1) + 128 * offset
-    degree = start[None] + jnp.arange(DEG, dtype=jnp.int32)[:, None, None]
-    big = (DEG, half, pairs_dev, 128)
-    coef_a = jnp.broadcast_to(ladder(degree, column_m[None])[..., None], big)
-    coef_b = jnp.broadcast_to((1.0 / ladder(degree - 1, column_m[None]))[..., None], big)
-    side = jnp.broadcast_to(on_second.astype(jnp.float32)[..., None], big[1:])
-    every_m = jnp.transpose(pair_m).reshape(cols)
     outer = width // INNER
-    coarse = INNER // FINE
-    fine_at = jnp.arange(FINE, dtype=jnp.int32)
-    coarse_at = FINE * jnp.arange(coarse, dtype=jnp.int32)
-    outer_at = rep * width + INNER * jnp.arange(outer, dtype=jnp.int32)
-    cos_all, sin_all = phases(every_m, jnp.concatenate([coarse_at, fine_at, outer_at]), period)
-    cut = lambda a: (a[:coarse], a[coarse:coarse + FINE], a[coarse + FINE:])
-    cos_a, cos_b, cos_o = cut(cos_all)
-    sin_a, sin_b, sin_o = cut(sin_all)
     vmem = pl.BlockSpec(memory_space=pltpu.VMEM)
-    out = jax.ShapeDtypeStruct((2, half, pairs_dev, DEG), jnp.float32)
-    sol, res = pl.pallas_call(
-        functools.partial(kernel, nb, scale),
+    hbm = pl.BlockSpec(memory_space=pl.ANY)
+    smem = pl.BlockSpec(memory_space=pltpu.SMEM)
+    out = jax.ShapeDtypeStruct(prior_weight.shape, jnp.float32)
+    f32 = lambda *shape: pltpu.VMEM(shape, jnp.float32)
+    b16 = lambda *shape: pltpu.VMEM(shape, jnp.bfloat16)
+    return pl.pallas_call(
+        functools.partial(kernel, nb, scale, period),
         out_shape=(out, out),
-        in_specs=[vmem] * 14,
+        in_specs=[hbm, hbm, vmem, vmem, vmem, vmem, smem],
         out_specs=(vmem, vmem),
         scratch_shapes=[
-            pltpu.VMEM((DEG, half, pairs_dev, rings), jnp.float32),
-            pltpu.VMEM((INNER, 2 * cols), jnp.bfloat16),
-            pltpu.VMEM((INNER, 2 * cols), jnp.bfloat16),
-            pltpu.VMEM((outer * rows, INNER), jnp.bfloat16),
-            pltpu.VMEM((outer * rows, INNER), jnp.bfloat16),
-            pltpu.VMEM((outer * rows, 2 * cols), jnp.bfloat16),
-            pltpu.VMEM((outer * rows, 2 * cols), jnp.bfloat16),
-            pltpu.VMEM((4, 2, half, pairs_dev, DEG), jnp.float32),
-            pltpu.VMEM((6, nb, 8, 128), jnp.float32),
-            pltpu.VMEM((6, 2 * nb, 8, 128), jnp.float32),
+            f32(rows, width),
+            f32(rows, width),
+            f32(DEG, half, pairs_dev, rings),
+            b16(INNER, 2 * cols),
+            b16(INNER, 2 * cols),
+            b16(outer * rows, INNER),
+            b16(outer * rows, INNER),
+            b16(outer * rows, 2 * cols),
+            b16(outer * rows, 2 * cols),
+            f32(INNER // FINE, cols),
+            f32(INNER // FINE, cols),
+            f32(FINE, cols),
+            f32(FINE, cols),
+            f32(outer, cols),
+            f32(outer, cols),
+            f32(pairs, 128),
+            f32(half, pairs_dev, 128),
+            f32(2, half, pairs_dev, DEG),
+            f32(4, 2, half, pairs_dev, DEG),
+            f32(6, nb, 8, 128),
+            f32(6, 2 * nb, 8, 128),
+            pltpu.SemaphoreType.DMA((2,)),
             pltpu.SemaphoreType.DMA((6,)),
             pltpu.SemaphoreType.DMA((6,)),
         ],
@@ -379,14 +464,9 @@
         ),
         name="wiener",
     )(
-        sky_map, noise_weight,
-        jnp.transpose(prior_weight, (2, 1, 0, 3)),
-        jnp.transpose(seeds, (2, 1, 0, 3)),
-        loop_cos[None, :],
-        coef_a, coef_b, side, cos_a, sin_a, cos_b, sin_b, cos_o, sin_o,
+        sky_map, noise_weight, prior_weight, seeds, loop_cos[None, :],
+        jnp.transpose(pair_m), block_count,
     )
-    back = lambda a: jnp.transpose(a, (2, 1, 0, 3))
-    return back(sol), back(res)
 
 
 def solution(mesh):

time: 76 us -> 60.4 us (0.79)
  local copies, waits for them, and re-layouts: 10.2 us -> 2.65 us
  Pallas kernels: 63.4 us -> 56.8 us
  other arithmetic: 1.37 us -> 0 us
    pallas_call x1, Pallas kernels: 63.4 us -> 56.8 us  [shards(): pl.pallas_call(functools.partial(kernel, nb, scale, period), out_shape=(o...]
    broadcast_in_dim x4 -> x0, local copies, waits for them, and re-layouts: 3.34 us -> none  [the longest x1 1.36 us: shards(): jnp.broadcast_to((1.0 / ladder(degree - 1, column_m[None]))[..., None], big)]
    slice x3 -> x0, local copies, waits for them, and re-layouts: 1.86 us -> none  [shards(): cut = lambda a: (a[:coarse], a[coarse:coarse + FINE], a[coarse + FINE:])]
    unnamed x12 -> x2, local copies, waits for them, and re-layouts: 3.93 us -> 2.65 us
    dynamic_slice x1 -> x0, local copies, waits for them, and re-layouts: 0.78 us -> none  [shards(): lax.dynamic_slice_in_dim(pair_m, lax.axis_index('blk') * pairs_dev, pairs...]
where the time goes in v2:
time: 60.4 us; the launch traced here: 60.1 us
  Pallas kernels  56.8 us (94%)
  local copies, waits for them, and re-layouts  2.65 us (4%)
  between operations  0.64 us (1%)
    pallas_call x1, Pallas kernels, shards(): pl.pallas_call(functools.partial(kernel, nb, scale, period), out_shape=(o...  56.8 us
    unnamed x2, local copies, waits for them, and re-layouts  2.65 us

profile of v2, /device:TPU:0, one launch (start us, length us, event | category | flops | bytes accessed | tf_op | source)
XLA Modules:
  0.0 60.1 jit_solution(4614086111871925729)
XLA Ops:
  0.6 56.8 %wiener.1 = (f32[8,2,2,128]{3,2,1,0:T(2,128)}, f32[8,2,2,128]{3,2,1,0:T(2,128)}) custom-call(f32[32,16384]{1,0:T(8,128)} %sky_in.1, f32[32,16384]{1,0:T(8,128)} %noise_in.1, f32[8,2,2,128]{3,2,1,0:T(2,128)} %prior_in.1, f32[8,2,2,512]{3,2,1,0:T(2,128)} %seeds.1, f32[1,512]{1,0:T(1,128)} %bitcast.2, s32[2,128]{1,0:T(2,128)} %bitcast.3, s32[8]{0:T(128)} %counts.1), custom_call_target="tpu_custom_call" | custom-call | tf_op jit(solution)/shard_map/wiener/pallas_call | solution.py:431
  57.4 1.3 %copy.11 = f32[8,2,2,128]{3,2,1,0:T(2,128)} copy(f32[8,2,2,128]{3,2,1,0:T(2,128)} %get-tuple-element.4) | data formatting | bytes 32768
  58.7 1.3 %copy.12 = f32[8,2,2,128]{3,2,1,0:T(2,128)} copy(f32[8,2,2,128]{3,2,1,0:T(2,128)} %get-tuple-element.5) | data formatting | bytes 32768

commit v3 on v2

--- a/solution.py
+++ b/solution.py
@@ -185,7 +185,9 @@
         dot = functools.partial(
             lax.dot_general, dimension_numbers=dims, preferred_element_type=jnp.float32
         )
-        return dot(a_hi, b_hi) + (dot(a_hi, b_lo) + dot(a_lo, b_hi))
+        both = dot(jnp.concatenate([a_hi, a_lo], axis=0), b_hi)
+        size = a_hi.shape[0]
+        return both[:size] + (both[size:] + dot(a_hi, b_lo))
 
     def forward(phase):
         def chunk(h, sums):

time: 60.4 us -> 60.4 us (level)
  no operation moved by 1% of the time
where the time goes in v3:
time: 60.4 us; the launch traced here: 60.1 us
  Pallas kernels  56.8 us (94%)
  local copies, waits for them, and re-layouts  2.65 us (4%)
  between operations  0.64 us (1%)
    pallas_call x1, Pallas kernels, shards(): pl.pallas_call(functools.partial(kernel, nb, scale, period), out_shape=(o...  56.8 us
    unnamed x2, local copies, waits for them, and re-layouts  2.65 us

profile of v3, /device:TPU:0, one launch (start us, length us, event | category | flops | bytes accessed | tf_op | source)
XLA Modules:
  0.0 60.1 jit_solution(8123722724438156479)
XLA Ops:
  0.6 56.8 %wiener.1 = (f32[8,2,2,128]{3,2,1,0:T(2,128)}, f32[8,2,2,128]{3,2,1,0:T(2,128)}) custom-call(f32[32,16384]{1,0:T(8,128)} %sky_in.1, f32[32,16384]{1,0:T(8,128)} %noise_in.1, f32[8,2,2,128]{3,2,1,0:T(2,128)} %prior_in.1, f32[8,2,2,512]{3,2,1,0:T(2,128)} %seeds.1, f32[1,512]{1,0:T(1,128)} %bitcast.2, s32[2,128]{1,0:T(2,128)} %bitcast.3, s32[8]{0:T(128)} %counts.1), custom_call_target="tpu_custom_call" | custom-call | tf_op jit(solution)/shard_map/wiener/pallas_call | solution.py:433
  57.4 1.3 %copy.11 = f32[8,2,2,128]{3,2,1,0:T(2,128)} copy(f32[8,2,2,128]{3,2,1,0:T(2,128)} %get-tuple-element.4) | data formatting | bytes 32768
  58.7 1.3 %copy.12 = f32[8,2,2,128]{3,2,1,0:T(2,128)} copy(f32[8,2,2,128]{3,2,1,0:T(2,128)} %get-tuple-element.5) | data formatting | bytes 32768

commit v4 on v3

--- a/solution.py
+++ b/solution.py
@@ -11,7 +11,6 @@
 DEG = 128
 INNER = 1024
 FINE = 32
-CHUNK = 8
 MESH = pl.DeviceIdType.MESH
 
 
@@ -26,30 +25,41 @@
     sol, res,
     sky, noise, legendre, basis_hi, basis_lo, pix_hi, pix_lo, st_hi, st_lo,
     cos_a, sin_a, cos_b, sin_b, cos_o, sin_o, by_pair, side, prior,
-    vecs, send, recv, load_sem, send_sem, recv_sem,
+    vecs, send, recv, gram_out, gram_in, load_sem, share_send, share_recv, send_sem, recv_sem,
 ):
-    rows, width = sky.shape
-    outer = width // INNER
+    _, rows, width = sky.shape
+    chunk = width // INNER
+    outer = 2 * chunk
     cols = cos_o.shape[1]
     pairs = cols // 2
     half = side.shape[0]
     rings = lcos.shape[1]
     groups = rings // 128
-    per = 128 // rows
     n = 2 * nb
     k = lax.axis_index("blk")
     c = lax.axis_index("rep")
-    me = c * nb + k
-    chunk_rows = CHUNK * rows
+    me = 2 * k + c
+    chunk_rows = chunk * rows
 
     def peer_of(d):
         peer = lax.rem(me + d, n)
-        return lax.rem(peer, nb), peer // nb
-
-    loads = [
-        pltpu.make_async_copy(sky_in, sky, load_sem.at[0]),
-        pltpu.make_async_copy(noise_in, noise, load_sem.at[1]),
-    ]
+        return peer // 2, lax.rem(peer, 2)
+
+    mine = pl.ds(pl.multiple_of(c * rows, rows), rows)
+    theirs = pl.ds(pl.multiple_of((1 - c) * rows, rows), rows)
+    loads, shares = [], []
+    for at, (src, dst) in enumerate(((sky_in, sky), (noise_in, noise))):
+        loads.append(pltpu.make_async_copy(src.at[mine, :], dst.at[c], load_sem.at[at]))
+        shares.append(
+            pltpu.make_async_remote_copy(
+                src_ref=src.at[theirs, :],
+                dst_ref=dst.at[c],
+                send_sem=share_send.at[at],
+                recv_sem=share_recv.at[at],
+                device_id=(k, 1 - c),
+                device_id_type=MESH,
+            )
+        )
     for load in loads:
         load.start()
     barrier = pltpu.get_barrier_semaphore()
@@ -61,25 +71,27 @@
 
     lax.fori_loop(1, n, greet, 0)
 
-    def post(phase, common):
+    def post(src, dst, at, spread_out):
+        pick = lambda pk, pc: 2 * pk + pc if spread_out else pk
+
         def one(d, _):
             pk, pc = peer_of(d)
             pltpu.make_async_remote_copy(
-                src_ref=send.at[phase, 0 if common else pk],
-                dst_ref=recv.at[phase, me],
-                send_sem=send_sem.at[phase],
-                recv_sem=recv_sem.at[phase],
+                src_ref=src.at[pick(pk, pc)],
+                dst_ref=dst.at[me],
+                send_sem=send_sem.at[at],
+                recv_sem=recv_sem.at[at],
                 device_id=(pk, pc),
                 device_id_type=MESH,
             ).start()
             return 0
 
         lax.fori_loop(1, n, one, 0)
-        recv[phase, me] = send[phase, 0 if common else k]
-
-    def drain(phase, sem):
-        block = recv.at[phase, pl.ds(0, n - 1)]
-        pltpu.make_async_copy(block, block, sem.at[phase]).wait()
+        dst[me] = src[pick(k, c)]
+
+    def drain(dst, at, sem):
+        block = dst.at[pl.ds(0, n - 1)]
+        pltpu.make_async_copy(block, block, sem.at[at]).wait()
 
     m_row = jnp.concatenate([every_m[0:1, :], every_m[1:2, :]], axis=1)
 
@@ -89,7 +101,10 @@
 
     trig(INNER // FINE, 0, FINE, cos_a, sin_a)
     trig(FINE, 0, 1, cos_b, sin_b)
-    trig(outer, c * width, INNER, cos_o, sin_o)
+    trig(outer, 0, INNER, cos_o, sin_o)
+    pl.semaphore_wait(barrier, n - 1)
+    for share in shares:
+        share.start()
 
     def make_basis(a, _):
         ca, sa = cos_a[pl.ds(a, 1), :], sin_a[pl.ds(a, 1), :]
@@ -105,18 +120,17 @@
 
     lax.fori_loop(0, INNER // FINE, make_basis, 0)
 
-    for load in loads:
-        load.wait()
-
-    def first_pixels(j, _):
-        lanes = pl.ds(pl.multiple_of(j * INNER, INNER), INNER)
-        hi, lo = split(sky[:, lanes] * noise[:, lanes])
-        where = pl.ds(pl.multiple_of(j * rows, rows), rows)
-        pix_hi[where, :] = hi
-        pix_lo[where, :] = lo
-        return 0
-
-    lax.fori_loop(0, outer, first_pixels, 0)
+    def first_pixels(side_id):
+        def one(j, _):
+            lanes = pl.ds(pl.multiple_of(j * INNER, INNER), INNER)
+            hi, lo = split(sky[side_id, :, lanes] * noise[side_id, :, lanes])
+            where = pl.ds(pl.multiple_of((side_id * chunk + j) * rows, rows), rows)
+            pix_hi[where, :] = hi
+            pix_lo[where, :] = lo
+            return 0
+
+        lax.fori_loop(0, chunk, one, 0)
+
     vecs[0] = jnp.zeros(vecs.shape[1:], jnp.float32)
 
     row_id = lax.broadcasted_iota(jnp.int32, (8, 128), 0)
@@ -127,9 +141,9 @@
         by_pair[...] = jnp.transpose(
             jnp.concatenate([m_float, jnp.zeros((126, pairs), jnp.float32)], axis=0)
         )
-        mine = by_pair[pl.ds(pl.multiple_of(k * 8, 8), 8), :]
-        m_first = jnp.broadcast_to(mine[:, 0:1], (8, 128)).astype(jnp.int32)
-        m_second = jnp.broadcast_to(mine[:, 1:2], (8, 128)).astype(jnp.int32)
+        local = by_pair[pl.ds(pl.multiple_of(k * 8, 8), 8), :]
+        m_first = jnp.broadcast_to(local[:, 0:1], (8, 128)).astype(jnp.int32)
+        m_second = jnp.broadcast_to(local[:, 1:2], (8, 128)).astype(jnp.int32)
         count = jnp.zeros((8, 128), jnp.int32)
         for p in range(8):
             count = jnp.where(row_id == p, counts[p], count)
@@ -189,17 +203,33 @@
         size = a_hi.shape[0]
         return both[:size] + (both[size:] + dot(a_hi, b_lo))
 
-    def forward(phase):
-        def chunk(h, sums):
+    def forward(it):
+        def half_of_loop(h, sums):
             re, im = sums
-            where = pl.ds(pl.multiple_of(h * chunk_rows, chunk_rows), chunk_rows)
+            part = lax.rem(h + c, 2)
+
+            @pl.when(it == 0)
+            def _():
+                @pl.when(h == 0)
+                def _():
+                    for load in loads:
+                        load.wait()
+
+                @pl.when(h == 1)
+                def _():
+                    for share in shares:
+                        share.wait_recv()
+
+                first_pixels(part)
+
+            where = pl.ds(pl.multiple_of(part * chunk_rows, chunk_rows), chunk_rows)
             sect = dots(
                 pix_hi[where, :], pix_lo[where, :], basis_hi[...], basis_lo[...],
                 (((1,), (0,)), ((), ())),
             )
-            for u in range(CHUNK):
-                co = cos_o[pl.ds(h * CHUNK + u, 1), :]
-                so = sin_o[pl.ds(h * CHUNK + u, 1), :]
+            for u in range(chunk):
+                co = cos_o[pl.ds(part * chunk + u, 1), :]
+                so = sin_o[pl.ds(part * chunk + u, 1), :]
                 cs = sect[u * rows:(u + 1) * rows, :cols]
                 ss = sect[u * rows:(u + 1) * rows, cols:]
                 re = re + (cs * co - ss * so)
@@ -207,14 +237,24 @@
             return re, im
 
         zero = jnp.zeros((rows, cols), jnp.float32)
-        re, im = lax.fori_loop(0, outer // CHUNK, chunk, (zero, zero))
+        re, im = lax.fori_loop(0, 2, half_of_loop, (zero, zero))
         stacked = scale * jnp.concatenate(
             [re[:, :pairs], im[:, :pairs], re[:, pairs:], im[:, pairs:]], axis=0
         )
-        send[phase] = jnp.transpose(stacked).reshape(nb, 8, 128)
+        stacked = jnp.transpose(
+            jnp.concatenate([stacked, jnp.zeros((64, pairs), jnp.float32)], axis=0)
+        )
+        for q in range(nb):
+            pack(send.at[2 * it, q], stacked[8 * q:8 * q + 8, :64])
+
+    def pack(ref, tile):
+        ref[...] = jnp.concatenate([tile[:4], tile[4:]], axis=1)
+
+    def unpack(tile):
+        return jnp.concatenate([tile[:, :64], tile[:, 64:]], axis=0)
 
     def spread(phase):
-        got = [recv[phase, q] + recv[phase, nb + q] for q in range(nb)]
+        got = [unpack(recv[phase, q]) for q in range(n)]
         gathered = []
         for part in range(4):
             at = part * rows
@@ -269,16 +309,19 @@
                     f = jnp.where(mask, f, 0.0) if s else jnp.where(mask, 0.0, f)
                     tot = f if tot is None else tot + f
                 parts.append(tot)
-        for q in range(nb):
-            send[phase, q] = jnp.concatenate(
+        for q in range(n):
+            pack(send.at[phase, q], jnp.concatenate(
                 [x[:, q * rows:(q + 1) * rows] for x in parts], axis=1
-            )
+            ))
 
     def inverse(phase):
-        table = (recv[phase, pl.ds(0, nb)] + recv[phase, pl.ds(nb, nb)]).reshape(pairs, 128)
+        table = jnp.concatenate(
+            [unpack(recv[phase, 2 * q] + recv[phase, 2 * q + 1]) for q in range(nb)], axis=0
+        )
+        table = jnp.concatenate([table, jnp.zeros((pairs, 64), jnp.float32)], axis=1)
         table = scale * jnp.transpose(table)
         re = jnp.concatenate([table[:rows], table[2 * rows:3 * rows]], axis=1)
-        im = jnp.concatenate([table[rows:2 * rows], table[3 * rows:]], axis=1)
+        im = jnp.concatenate([table[rows:2 * rows], table[3 * rows:4 * rows]], axis=1)
 
         def mix(j, _):
             co, so = cos_o[pl.ds(j, 1), :], sin_o[pl.ds(j, 1), :]
@@ -293,15 +336,15 @@
 
         lax.fori_loop(0, outer, mix, 0)
 
-        def chunk(h, energy):
+        def half_of_loop(h, energy):
             where = pl.ds(pl.multiple_of(h * chunk_rows, chunk_rows), chunk_rows)
             pix = dots(
                 st_hi[where, :], st_lo[where, :], basis_hi[...], basis_lo[...],
                 (((1,), (1,)), ((), ())),
             )
-            for u in range(CHUNK):
-                j = h * CHUNK + u
-                weight = noise[:, pl.ds(pl.multiple_of(j * INNER, INNER), INNER)]
+            for u in range(chunk):
+                j = h * chunk + u
+                weight = noise[h, :, u * INNER:(u + 1) * INNER]
                 values = pix[u * rows:(u + 1) * rows]
                 weighted = weight * values
                 power = weighted * values
@@ -313,23 +356,37 @@
                 pix_lo[at, :] = lo
             return energy
 
-        return lax.fori_loop(0, outer // CHUNK, chunk, jnp.zeros((rows, 128), jnp.float32))
+        return lax.fori_loop(0, 2, half_of_loop, jnp.zeros((rows, 128), jnp.float32))
 
     def dot_lanes(a, b):
         x = (a * b).reshape(4, 8, 128)
         return jnp.sum(x[0] + x[1] + (x[2] + x[3]), axis=0, keepdims=True)
 
-    pl.semaphore_wait(barrier, n - 1)
+    def post_gram():
+        def one(d, _):
+            pk, pc = peer_of(d)
+            pltpu.make_async_remote_copy(
+                src_ref=gram_out.at[0],
+                dst_ref=gram_in.at[me],
+                send_sem=send_sem.at[5],
+                recv_sem=recv_sem.at[5],
+                device_id=(pk, pc),
+                device_id_type=MESH,
+            ).start()
+            return 0
+
+        lax.fori_loop(1, n, one, 0)
+        gram_in[me] = gram_out[0]
 
     def turn(it, _):
-        forward(2 * it)
-        post(2 * it, False)
+        forward(it)
+        post(send.at[2 * it], recv.at[2 * it], 2 * it, False)
 
         @pl.when(it == 0)
         def _():
             make_legendre()
 
-        drain(2 * it, recv_sem)
+        drain(recv.at[2 * it], 2 * it, recv_sem)
         out = spread(2 * it)
         vec = []
         for t in range(2):
@@ -340,19 +397,19 @@
         @pl.when(it < 2)
         def _():
             gather_columns(vec, 2 * it + 1)
-            post(2 * it + 1, False)
-            drain(2 * it + 1, recv_sem)
+            post(send.at[2 * it + 1], recv.at[2 * it + 1], 2 * it + 1, True)
+            drain(recv.at[2 * it + 1], 2 * it + 1, recv_sem)
             energy = inverse(2 * it + 1)
 
             @pl.when(it == 1)
             def _():
                 v0, v1 = vecs[1], vecs[2]
                 bent = dot_lanes(v1, prior[...] * v1) + jnp.sum(energy, axis=0, keepdims=True)
-                send[5, 0] = jnp.concatenate(
+                gram_out[0] = jnp.concatenate(
                     [dot_lanes(v0, v0), dot_lanes(v0, v1), dot_lanes(v1, v1), bent,
                      jnp.zeros((4, 128), jnp.float32)], axis=0
                 )
-                post(5, True)
+                post_gram()
 
         return 0
 
@@ -360,8 +417,8 @@
 
     v0, v1, v2 = vecs[1], vecs[2], vecs[3]
 
-    drain(5, recv_sem)
-    gram = jnp.sum(jnp.sum(recv[5], axis=0), axis=1, keepdims=True)
+    drain(gram_in, 5, recv_sem)
+    gram = jnp.sum(jnp.sum(gram_in[...], axis=0), axis=1, keepdims=True)
     bb, bv, vv, vw = (gram[q:q + 1] for q in range(4))
     alpha = bb / bv
     norm = bb - 2.0 * alpha * bv + alpha * alpha * vv
@@ -381,10 +438,13 @@
                 res[p, b, t:t + 1, :] = left[p:p + 1]
 
     def finish(phase, _):
-        drain(phase, send_sem)
+        drain(recv.at[phase], phase, send_sem)
         return 0
 
-    lax.fori_loop(0, 6, finish, 0)
+    lax.fori_loop(0, 5, finish, 0)
+    drain(gram_in, 5, send_sem)
+    for share in shares:
+        share.wait_send()
 
 
 def ladder(degree, column_m):
@@ -423,7 +483,8 @@
     rows, width = sky_map.shape
     period = width * lax.axis_size("rep")
     scale = 1.0 / math.sqrt(rings * period)
-    outer = width // INNER
+    rows = rows // 2
+    outer = period // INNER
     vmem = pl.BlockSpec(memory_space=pltpu.VMEM)
     hbm = pl.BlockSpec(memory_space=pl.ANY)
     smem = pl.BlockSpec(memory_space=pltpu.SMEM)
@@ -436,8 +497,8 @@
         in_specs=[hbm, hbm, vmem, vmem, vmem, vmem, smem],
         out_specs=(vmem, vmem),
         scratch_shapes=[
-            f32(rows, width),
-            f32(rows, width),
+            f32(2, rows, width),
+            f32(2, rows, width),
             f32(DEG, half, pairs_dev, rings),
             b16(INNER, 2 * cols),
             b16(INNER, 2 * cols),
@@ -455,8 +516,12 @@
             f32(half, pairs_dev, 128),
             f32(2, half, pairs_dev, DEG),
             f32(4, 2, half, pairs_dev, DEG),
-            f32(6, nb, 8, 128),
-            f32(6, 2 * nb, 8, 128),
+            f32(5, 2 * nb, 4, 128),
+            f32(5, 2 * nb, 4, 128),
+            f32(1, 8, 128),
+            f32(2 * nb, 8, 128),
+            pltpu.SemaphoreType.DMA((2,)),
+            pltpu.SemaphoreType.DMA((2,)),
             pltpu.SemaphoreType.DMA((2,)),
             pltpu.SemaphoreType.DMA((6,)),
             pltpu.SemaphoreType.DMA((6,)),

time: 60.4 us -> 61.9 us (1.025)
  Pallas kernels: 56.8 us -> 58.2 us
    pallas_call x1, Pallas kernels: 56.8 us -> 58.2 us  [shards(): pl.pallas_call(functools.partial(kernel, nb, scale, period), out_shape=(o...]
where the time goes in v4:
time: 61.9 us; the launch traced here: 61.5 us
  Pallas kernels  58.2 us (94%)
  local copies, waits for them, and re-layouts  2.65 us (4%)
  between operations  0.64 us (1%)
    pallas_call x1, Pallas kernels, shards(): pl.pallas_call(functools.partial(kernel, nb, scale, period), out_shape=(o...  58.2 us
    unnamed x2, local copies, waits for them, and re-layouts  2.65 us

profile of v4, /device:TPU:0, one launch (start us, length us, event | category | flops | bytes accessed | tf_op | source)
XLA Modules:
  0.0 61.5 jit_solution(8039420153551483566)
XLA Ops:
  0.6 58.2 %wiener.1 = (f32[8,2,2,128]{3,2,1,0:T(2,128)}, f32[8,2,2,128]{3,2,1,0:T(2,128)}) custom-call(f32[32,16384]{1,0:T(8,128)} %sky_in.1, f32[32,16384]{1,0:T(8,128)} %noise_in.1, f32[8,2,2,128]{3,2,1,0:T(2,128)} %prior_in.1, f32[8,2,2,512]{3,2,1,0:T(2,128)} %seeds.1, f32[1,512]{1,0:T(1,128)} %bitcast.2, s32[2,128]{1,0:T(2,128)} %bitcast.3, s32[8]{0:T(128)} %counts.1), custom_call_target="tpu_custom_call" | custom-call | tf_op jit(solution)/shard_map/wiener/pallas_call | solution.py:494
  58.9 1.3 %copy.11 = f32[8,2,2,128]{3,2,1,0:T(2,128)} copy(f32[8,2,2,128]{3,2,1,0:T(2,128)} %get-tuple-element.4) | data formatting | bytes 32768
  60.2 1.3 %copy.12 = f32[8,2,2,128]{3,2,1,0:T(2,128)} copy(f32[8,2,2,128]{3,2,1,0:T(2,128)} %get-tuple-element.5) | data formatting | bytes 32768

commit v5 on v2

--- a/solution.py
+++ b/solution.py
@@ -23,7 +23,7 @@
 def kernel(
     nb, scale, period,
     sky_in, noise_in, prior_in, seeds, lcos, every_m, counts,
-    sol, res,
+    both,
     sky, noise, legendre, basis_hi, basis_lo, pix_hi, pix_lo, st_hi, st_lo,
     cos_a, sin_a, cos_b, sin_b, cos_o, sin_o, by_pair, side, prior,
     vecs, send, recv, load_sem, send_sem, recv_sem,
@@ -42,9 +42,20 @@
     me = c * nb + k
     chunk_rows = CHUNK * rows
 
-    def peer_of(d):
-        peer = lax.rem(me + d, n)
-        return lax.rem(peer, nb), peer // nb
+    unroll = 5 if (nb - 1) % 5 == 0 else 3 if (nb - 1) % 3 == 0 else 1
+
+    def each_peer(visit):
+        visit(k, 1 - c)
+
+        def some(g, _):
+            for u in range(unroll):
+                pk = k + g * unroll + (u + 1)
+                pk = jnp.where(pk >= nb, pk - nb, pk)
+                visit(pk, c)
+                visit(pk, 1 - c)
+            return 0
+
+        lax.fori_loop(0, (nb - 1) // unroll, some, 0)
 
     loads = [
         pltpu.make_async_copy(sky_in, sky, load_sem.at[0]),
@@ -54,16 +65,13 @@
         load.start()
     barrier = pltpu.get_barrier_semaphore()
 
-    def greet(d, _):
-        pk, pc = peer_of(d)
+    def greet(pk, pc):
         pl.semaphore_signal(barrier, inc=1, device_id=(pk, pc), device_id_type=MESH)
-        return 0
-
-    lax.fori_loop(1, n, greet, 0)
+
+    each_peer(greet)
 
     def post(phase, common):
-        def one(d, _):
-            pk, pc = peer_of(d)
+        def one(pk, pc):
             pltpu.make_async_remote_copy(
                 src_ref=send.at[phase, 0 if common else pk],
                 dst_ref=recv.at[phase, me],
@@ -72,9 +80,8 @@
                 device_id=(pk, pc),
                 device_id_type=MESH,
             ).start()
-            return 0
-
-        lax.fori_loop(1, n, one, 0)
+
+        each_peer(one)
         recv[phase, me] = send[phase, 0 if common else k]
 
     def drain(phase, sem):
@@ -182,10 +189,13 @@
         lax.fori_loop(1, DEG // 8, step, (tuple(coefs), tuple(state)))
 
     def dots(a_hi, a_lo, b_hi, b_lo, dims):
-        dot = functools.partial(
-            lax.dot_general, dimension_numbers=dims, preferred_element_type=jnp.float32
+        depth = dims[0][1][0]
+        return lax.dot_general(
+            jnp.concatenate([a_hi, a_lo, a_hi], axis=1),
+            jnp.concatenate([b_hi, b_hi, b_lo], axis=depth),
+            dimension_numbers=dims,
+            preferred_element_type=jnp.float32,
         )
-        return dot(a_hi, b_hi) + (dot(a_hi, b_lo) + dot(a_lo, b_hi))
 
     def forward(phase):
         def chunk(h, sums):
@@ -375,14 +385,19 @@
             found = alpha * b0 + alpha2 * d1
             left = r1 - alpha2 * (more * b1 - alpha * b2)
             for p in range(8):
-                sol[p, b, t:t + 1, :] = found[p:p + 1]
-                res[p, b, t:t + 1, :] = left[p:p + 1]
+                both[0, p, b, t:t + 1, :] = found[p:p + 1]
+                both[1, p, b, t:t + 1, :] = left[p:p + 1]
 
     def finish(phase, _):
         drain(phase, send_sem)
         return 0
 
     lax.fori_loop(0, 6, finish, 0)
+
+
+def unpack_kernel(both, sol, res):
+    sol[...] = both[0]
+    res[...] = both[1]
 
 
 def ladder(degree, column_m):
@@ -428,11 +443,11 @@
     out = jax.ShapeDtypeStruct(prior_weight.shape, jnp.float32)
     f32 = lambda *shape: pltpu.VMEM(shape, jnp.float32)
     b16 = lambda *shape: pltpu.VMEM(shape, jnp.bfloat16)
-    return pl.pallas_call(
+    both = pl.pallas_call(
         functools.partial(kernel, nb, scale, period),
-        out_shape=(out, out),
+        out_shape=jax.ShapeDtypeStruct((2,) + prior_weight.shape, jnp.float32),
         in_specs=[hbm, hbm, vmem, vmem, vmem, vmem, smem],
-        out_specs=(vmem, vmem),
+        out_specs=vmem,
         scratch_shapes=[
             f32(rows, width),
             f32(rows, width),
@@ -467,6 +482,13 @@
         sky_map, noise_weight, prior_weight, seeds, loop_cos[None, :],
         jnp.transpose(pair_m), block_count,
     )
+    return pl.pallas_call(
+        unpack_kernel,
+        out_shape=(out, out),
+        in_specs=[vmem],
+        out_specs=(vmem, vmem),
+        name="outputs",
+    )(both)
 
 
 def solution(mesh):

time: 60.4 us -> 58.4 us (0.967)
  local copies, waits for them, and re-layouts: 2.65 us -> 0 us
  Pallas kernels: 56.8 us -> 57.6 us
    unnamed x2 -> x0, local copies, waits for them, and re-layouts: 2.65 us -> none
    pallas_call x1 -> x2, Pallas kernels: 56.8 us -> 57.6 us  [the longest x1 56.2 us: shards(): pl.pallas_call(functools.partial(kernel, nb, scale, period), out_shape=ja...]
where the time goes in v5:
time: 58.4 us; the launch traced here: 58.2 us
  Pallas kernels  57.6 us (99%)
  between operations  0.64 us (1%)
    pallas_call x1, Pallas kernels, shards(): pl.pallas_call(functools.partial(kernel, nb, scale, period), out_shape=ja...  56.2 us
    pallas_call x1, Pallas kernels, shards(): pl.pallas_call(unpack_kernel, out_shape=(out, out), in_specs=[vmem], out_...  1.37 us

profile of v5, /device:TPU:0, one launch (start us, length us, event | category | flops | bytes accessed | tf_op | source)
XLA Modules:
  0.0 58.2 jit_solution(7356161046318262887)
XLA Ops:
  0.6 56.2 %wiener.1.both = f32[2,8,2,2,128]{4,3,2,1,0:T(2,128)} custom-call(f32[32,16384]{1,0:T(8,128)} %sky_in.1, f32[32,16384]{1,0:T(8,128)} %noise_in.1, f32[8,2,2,128]{3,2,1,0:T(2,128)} %prior_in.1, f32[8,2,2,512]{3,2,1,0:T(2,128)} %seeds.1, f32[1,512]{1,0:T(1,128)} %bitcast.2, s32[2,128]{1,0:T(2,128)} %bitcast.3, s32[8]{0:T(128)} %counts.1), custom_call_target="tpu_custom_call" | custom-call | tf_op jit(solution)/shard_map/wiener/pallas_call | solution.py:446
  56.8 1.4 %outputs.1 = (f32[8,2,2,128]{3,2,1,0:T(2,128)}, f32[8,2,2,128]{3,2,1,0:T(2,128)}) custom-call(f32[2,8,2,2,128]{4,3,2,1,0:T(2,128)} %wiener.1.both), custom_call_target="tpu_custom_call" | custom-call | tf_op jit(solution)/shard_map/outputs/pallas_call | solution.py:485

commit v6 on v5

--- a/solution.py
+++ b/solution.py
@@ -35,6 +35,7 @@
     half = side.shape[0]
     rings = lcos.shape[1]
     groups = rings // 128
+    batch = 32 if groups <= 4 else 8
     per = 128 // rows
     n = 2 * nb
     k = lax.axis_index("blk")
@@ -176,17 +177,17 @@
             return out
 
         coefs = [v for pair in coefs for v in pair]
-        for i in range(2, 8):
+        for i in range(2, batch):
             state = advance(i, i, coefs, state)
 
         def step(g, packed):
             coefs, state = packed
-            coefs = tuple(pltpu.roll(v, 120, 1) for v in coefs)
-            for u in range(8):
-                state = advance(g * 8 + u, u, coefs, state)
+            coefs = tuple(pltpu.roll(v, 128 - batch, 1) for v in coefs)
+            for u in range(batch):
+                state = advance(g * batch + u, u, coefs, state)
             return coefs, tuple(state)
 
-        lax.fori_loop(1, DEG // 8, step, (tuple(coefs), tuple(state)))
+        lax.fori_loop(1, DEG // batch, step, (tuple(coefs), tuple(state)))
 
     def dots(a_hi, a_lo, b_hi, b_lo, dims):
         depth = dims[0][1][0]
@@ -237,8 +238,8 @@
 
         def step(g, acc):
             acc = list(acc)
-            for u in range(8):
-                i = g * 8 + u
+            for u in range(batch):
+                i = g * batch + u
                 for b in range(2):
                     leg = legendre[i, b]
                     for t in range(2):
@@ -251,22 +252,22 @@
             return tuple(acc)
 
         zero = jnp.zeros((8, 128), jnp.float32)
-        return lax.fori_loop(0, DEG // 8, step, (zero,) * 4)
+        return lax.fori_loop(0, DEG // batch, step, (zero,) * 4)
 
     def gather_columns(vec, phase):
         def step(g, packed):
             coef, acc = packed
             acc = list(acc)
-            for u in range(8):
+            for u in range(batch):
                 for b in range(2):
-                    leg = legendre[g * 8 + u, b]
+                    leg = legendre[g * batch + u, b]
                     for t in range(2):
                         acc[2 * t + b] = acc[2 * t + b] + leg * coef[2 * t + b][:, u:u + 1]
-            coef = tuple(pltpu.roll(x, 120, 1) for x in coef)
+            coef = tuple(pltpu.roll(x, 128 - batch, 1) for x in coef)
             return coef, tuple(acc)
 
         zero = jnp.zeros((8, rings), jnp.float32)
-        _, acc = lax.fori_loop(0, DEG // 8, step, (tuple(vec), (zero,) * 4))
+        _, acc = lax.fori_loop(0, DEG // batch, step, (tuple(vec), (zero,) * 4))
         parts = []
         for s in range(2):
             for t in range(2):

time: 58.4 us -> 54 us (0.925)
  Pallas kernels: 57.6 us -> 53.1 us
    pallas_call x1, Pallas kernels: 56.2 us -> 51.7 us  [shards(): pl.pallas_call(functools.partial(kernel, nb, scale, period), out_shape=ja...]
where the time goes in v6:
time: 54 us; the launch traced here: 53.7 us
  Pallas kernels  53.1 us (98%)
  between operations  0.64 us (1%)
    pallas_call x1, Pallas kernels, shards(): pl.pallas_call(functools.partial(kernel, nb, scale, period), out_shape=ja...  51.7 us
    pallas_call x1, Pallas kernels, shards(): pl.pallas_call(unpack_kernel, out_shape=(out, out), in_specs=[vmem], out_...  1.37 us

profile of v6, /device:TPU:0, one launch (start us, length us, event | category | flops | bytes accessed | tf_op | source)
XLA Modules:
  0.0 53.7 jit_solution(14352158795451406831)
XLA Ops:
  0.6 51.7 %wiener.1.both = f32[2,8,2,2,128]{4,3,2,1,0:T(2,128)} custom-call(f32[32,16384]{1,0:T(8,128)} %sky_in.1, f32[32,16384]{1,0:T(8,128)} %noise_in.1, f32[8,2,2,128]{3,2,1,0:T(2,128)} %prior_in.1, f32[8,2,2,512]{3,2,1,0:T(2,128)} %seeds.1, f32[1,512]{1,0:T(1,128)} %bitcast.2, s32[2,128]{1,0:T(2,128)} %bitcast.3, s32[8]{0:T(128)} %counts.1), custom_call_target="tpu_custom_call" | custom-call | tf_op jit(solution)/shard_map/wiener/pallas_call | solution.py:447
  52.4 1.4 %outputs.1 = (f32[8,2,2,128]{3,2,1,0:T(2,128)}, f32[8,2,2,128]{3,2,1,0:T(2,128)}) custom-call(f32[2,8,2,2,128]{4,3,2,1,0:T(2,128)} %wiener.1.both), custom_call_target="tpu_custom_call" | custom-call | tf_op jit(solution)/shard_map/outputs/pallas_call | solution.py:486

commit v7 on v6

--- a/solution.py
+++ b/solution.py
@@ -35,7 +35,7 @@
     half = side.shape[0]
     rings = lcos.shape[1]
     groups = rings // 128
-    batch = 32 if groups <= 4 else 8
+    batch = 64 if groups <= 4 else 8
     per = 128 // rows
     n = 2 * nb
     k = lax.axis_index("blk")
@@ -65,6 +65,14 @@
     for load in loads:
         load.start()
     barrier = pltpu.get_barrier_semaphore()
+
+    def in_fours(count, visit):
+        def four(g, _):
+            for u in range(4):
+                visit(g * 4 + u)
+            return 0
+
+        lax.fori_loop(0, count // 4, four, 0)
 
     def greet(pk, pc):
         pl.semaphore_signal(barrier, inc=1, device_id=(pk, pc), device_id_type=MESH)
@@ -99,7 +107,7 @@
     trig(FINE, 0, 1, cos_b, sin_b)
     trig(outer, c * width, INNER, cos_o, sin_o)
 
-    def make_basis(a, _):
+    def make_basis(a):
         ca, sa = cos_a[pl.ds(a, 1), :], sin_a[pl.ds(a, 1), :]
         cb, sb = cos_b[...], sin_b[...]
         where = pl.ds(pl.multiple_of(a * FINE, FINE), FINE)
@@ -109,9 +117,8 @@
         hi, lo = split(sa * cb + ca * sb)
         basis_hi[where, cols:] = hi
         basis_lo[where, cols:] = lo
-        return 0
-
-    lax.fori_loop(0, INNER // FINE, make_basis, 0)
+
+    in_fours(INNER // FINE, make_basis)
 
     for load in loads:
         load.wait()
@@ -289,7 +296,7 @@
         re = jnp.concatenate([table[:rows], table[2 * rows:3 * rows]], axis=1)
         im = jnp.concatenate([table[rows:2 * rows], table[3 * rows:]], axis=1)
 
-        def mix(j, _):
+        def mix(j):
             co, so = cos_o[pl.ds(j, 1), :], sin_o[pl.ds(j, 1), :]
             where = pl.ds(pl.multiple_of(j * rows, rows), rows)
             hi, lo = split(re * co - im * so)
@@ -298,9 +305,8 @@
             hi, lo = split(-(re * so + im * co))
             st_hi[where, cols:] = hi
             st_lo[where, cols:] = lo
-            return 0
-
-        lax.fori_loop(0, outer, mix, 0)
+
+        in_fours(outer, mix)
 
         def chunk(h, energy):
             where = pl.ds(pl.multiple_of(h * chunk_rows, chunk_rows), chunk_rows)

time: 54 us -> 53.3 us (0.987)
  Pallas kernels: 53.1 us -> 52.4 us
    pallas_call x1, Pallas kernels: 51.7 us -> 51 us  [shards(): pl.pallas_call(functools.partial(kernel, nb, scale, period), out_shape=ja...]
where the time goes in v7:
time: 53.3 us; the launch traced here: 53 us
  Pallas kernels  52.4 us (98%)
  between operations  0.64 us (1%)
    pallas_call x1, Pallas kernels, shards(): pl.pallas_call(functools.partial(kernel, nb, scale, period), out_shape=ja...  51 us
    pallas_call x1, Pallas kernels, shards(): pl.pallas_call(unpack_kernel, out_shape=(out, out), in_specs=[vmem], out_...  1.37 us

profile of v7, /device:TPU:0, one launch (start us, length us, event | category | flops | bytes accessed | tf_op | source)
XLA Modules:
  0.0 53.0 jit_solution(18340262609382529184)
XLA Ops:
  0.6 51.0 %wiener.1.both = f32[2,8,2,2,128]{4,3,2,1,0:T(2,128)} custom-call(f32[32,16384]{1,0:T(8,128)} %sky_in.1, f32[32,16384]{1,0:T(8,128)} %noise_in.1, f32[8,2,2,128]{3,2,1,0:T(2,128)} %prior_in.1, f32[8,2,2,512]{3,2,1,0:T(2,128)} %seeds.1, f32[1,512]{1,0:T(1,128)} %bitcast.2, s32[2,128]{1,0:T(2,128)} %bitcast.3, s32[8]{0:T(128)} %counts.1), custom_call_target="tpu_custom_call" | custom-call | tf_op jit(solution)/shard_map/wiener/pallas_call | solution.py:453
  51.6 1.4 %outputs.1 = (f32[8,2,2,128]{3,2,1,0:T(2,128)}, f32[8,2,2,128]{3,2,1,0:T(2,128)}) custom-call(f32[2,8,2,2,128]{4,3,2,1,0:T(2,128)} %wiener.1.both), custom_call_target="tpu_custom_call" | custom-call | tf_op jit(solution)/shard_map/outputs/pallas_call | solution.py:492
